TPU v7x, 768 devices: a whole 4x8x12 slice. The times are simulated.
768 devices in a mesh: seq: 24 (over z, core), ctx: 32 (over x, y).
Axes of the slice: x: 4, y: 8, z: 12, core: 2. Of those that a mesh axis runs over, the one named last changes fastest.
Arguments:
- tokens: bfloat16 [98304, 2048], P(('seq', 'ctx')), parts along dimension 0, may hold values from -14 to 14
- queries: bfloat16 [98304, 2048], P(('seq', 'ctx')), parts along dimension 0, may hold values from -10 to 10
- keys: bfloat16 [98304, 512], P(('seq', 'ctx')), parts along dimension 0, may hold values from -10 to 10
- values: bfloat16 [98304, 512], P(('seq', 'ctx')), parts along dimension 0, may hold values from -6 to 6
- norm_gain: bfloat16 [2048], replicated, may hold values from 0.5 to 1.5
- router: bfloat16 [2048, 32], replicated, may hold values from -0.375 to 0.375
- w_gate: bfloat16 [32, 2048, 512], P('ctx'), may hold values from -0.125 to 0.125
- w_up: bfloat16 [32, 2048, 512], P('ctx'), may hold values from -0.125 to 0.125
- w_down: bfloat16 [32, 512, 2048], P('ctx'), may hold values from -0.25 to 0.25
- picks: int32 [98304, 2], P(('seq', 'ctx')), parts along dimension 0, may hold values from 0 to 31, all different within a row
Outputs:
- layer: bfloat16 [98304, 2048], P(('seq', 'ctx')), parts along dimension 0
There are 24 independent parts, one for each index of `seq`. A program takes and returns all parts, laid end to end along the dimension named above; an argument that names none is the same for every part. Nothing has to cross between parts.
All inputs are finite; a program needn't handle non-finite values.
Results may differ from a plain program's by a relative error of at most 0.0054.
Values may be sent and summed in bfloat16 or wider, within the bound.
A program may use at most 64 MiB of HBM per device.

v0:
```python
import math

import jax
import jax.numpy as jnp
from jax import lax
from jax.sharding import PartitionSpec as P

HEADS = 16
KV_HEADS = 4
HEAD_DIM = 128
ITERS = 8


score_cap = 50.0
logit_cap = 10.0
epsilon = 1e-06


def key_block_loop(query_heads, positions, latest, key_rows, value_rows, block_size):

    def advance(block_index, running):
        key_first = block_index * block_size

        def compute(current):
            summed, denom = current
            key_block = lax.dynamic_slice_in_dim(key_rows, key_first, block_size, 0)
            value_block = lax.dynamic_slice_in_dim(value_rows, key_first, block_size, 0)
            scores = jnp.einsum(
                "tkgd,rkd->kgtr", query_heads, key_block, preferred_element_type=jnp.float32
            ) / math.sqrt(HEAD_DIM)
            weights = jnp.exp(score_cap * jnp.tanh(scores / score_cap))
            key_positions = key_first + jnp.arange(block_size, dtype=jnp.int32)
            visible = key_positions[None, None, None, :] <= positions[None, None, :, None]
            weights = jnp.where(visible, weights, 0.0)
            denom = denom + jnp.sum(weights, -1)
            summed = summed + jnp.einsum(
                "kgtr,rkd->tkgd",
                weights.astype(jnp.bfloat16),
                value_block,
                preferred_element_type=jnp.float32,
            )
            return (summed, denom)

        def unchanged(current):
            return current

        return lax.cond(key_first <= latest, compute, unchanged, running)

    return advance


def attend(query_sets, keys, values):
    group = HEADS // KV_HEADS
    prepared = []
    initial = []
    for query_rows, positions in query_sets:
        length = query_rows.shape[0]
        prepared.append(
            (query_rows.reshape(length, KV_HEADS, group, HEAD_DIM), positions, jnp.max(positions))
        )
        initial.append(
            (
                jnp.zeros((length, KV_HEADS, group, HEAD_DIM), jnp.float32),
                jnp.zeros((KV_HEADS, group, length), jnp.float32),
            )
        )
    running = tuple(initial)
    key_piece = lax.all_gather(keys, "ctx", axis=0, tiled=True)
    value_piece = lax.all_gather(values, "ctx", axis=0, tiled=True)
    piece_rows = key_piece.shape[0]
    block_size = math.gcd(piece_rows, 512)
    key_rows = key_piece.reshape(piece_rows, KV_HEADS, HEAD_DIM)
    value_rows = value_piece.reshape(piece_rows, KV_HEADS, HEAD_DIM)
    updated = []
    for (query_heads, positions, latest), current in zip(prepared, running):
        advance = key_block_loop(query_heads, positions, latest, key_rows, value_rows, block_size)
        updated.append(lax.fori_loop(0, piece_rows // block_size, advance, current))
    finished = tuple(updated)
    results = []
    for summed, denom in finished:
        normal_out = summed / jnp.transpose(denom, (2, 0, 1))[..., None]
        results.append(normal_out.reshape(summed.shape[0], -1).astype(jnp.bfloat16))
    return results


def per_device(tokens, queries, keys, values, norm_gain, router, w_gate, w_up, w_down, picks):
    devices = lax.axis_size("ctx")
    my_index = lax.axis_index("ctx")
    my_rows = tokens.shape[0]
    offsets = jnp.arange(my_rows, dtype=jnp.int32) + my_index * my_rows
    attended = attend([(queries, offsets)], keys, values)[0]
    stream = (
        (tokens.astype(jnp.float32) + attended.astype(jnp.float32))
        .astype(jnp.bfloat16)
        .astype(jnp.float32)
    )
    mean_square = jnp.mean(stream * stream, -1, keepdims=True)
    normed = (stream * lax.rsqrt(mean_square + epsilon) * norm_gain.astype(jnp.float32)).astype(
        jnp.bfloat16
    )
    logits = logit_cap * jnp.tanh(
        jnp.dot(normed, router, preferred_element_type=jnp.float32) / logit_cap
    )
    plan = jnp.exp(logits)
    plan = plan / jnp.sum(plan, -1, keepdims=True)
    experts = router.shape[1]
    top_count = picks.shape[1]
    capacity = max(2, my_rows * top_count // experts)
    target = my_rows * devices * top_count / experts
    for sweep in range(ITERS):
        columns = lax.psum(jnp.sum(plan, 0), "ctx")
        plan = plan * (target / columns)
        plan = plan * (top_count / jnp.sum(plan, -1, keepdims=True))
    chooses = picks[:, :, None] == jnp.arange(experts, dtype=jnp.int32)[None, None, :]
    chosen = jnp.sum(jnp.where(chooses, plan[:, None, :], 0.0), -1)
    gates = chosen / jnp.sum(chosen, -1, keepdims=True)
    flags = chooses.reshape(my_rows * top_count, experts).astype(jnp.int32)
    ranks = jnp.cumsum(flags, 0) - flags
    slots = jnp.sum(ranks * flags, -1).reshape(my_rows, top_count)
    kept = slots < capacity
    targets = picks * capacity + jnp.minimum(slots, capacity - 1)
    slot_ids = jnp.arange(experts * capacity, dtype=jnp.int32)
    selected = jnp.any(
        (slot_ids[:, None, None] == targets[None, :, :]) & kept[None, :, :], -1
    ).astype(jnp.bfloat16)
    outgoing = jnp.dot(selected, normed, preferred_element_type=jnp.float32).astype(jnp.bfloat16)
    local_experts = w_gate.shape[0]
    outgoing = outgoing.reshape(devices, local_experts, capacity, normed.shape[1])
    incoming = lax.all_to_all(outgoing, "ctx", split_axis=0, concat_axis=0, tiled=True)
    gate = jnp.einsum("secd,edf->secf", incoming, w_gate, preferred_element_type=jnp.float32)
    upward = jnp.einsum("secd,edf->secf", incoming, w_up, preferred_element_type=jnp.float32)
    hidden = (jax.nn.silu(gate) * upward).astype(jnp.bfloat16)
    processed = jnp.einsum(
        "secf,efd->secd", hidden, w_down, preferred_element_type=jnp.float32
    ).astype(jnp.bfloat16)
    back_rows = lax.all_to_all(processed, "ctx", split_axis=0, concat_axis=0, tiled=True)
    flat_back = back_rows.reshape(experts * capacity, normed.shape[1])
    gathered = flat_back[targets]
    scale = jnp.where(kept, gates, 0.0)
    mixture = jnp.sum(gathered.astype(jnp.float32) * scale[:, :, None], 1)
    return (stream + mixture).astype(jnp.bfloat16)


def solution(mesh):
    placed = (
        P(("seq", "ctx"), None),
        P(("seq", "ctx"), None),
        P(("seq", "ctx"), None),
        P(("seq", "ctx"), None),
        P(),
        P(),
        P("ctx", None, None),
        P("ctx", None, None),
        P("ctx", None, None),
        P(("seq", "ctx"), None),
    )
    return jax.shard_map(
        per_device, mesh=mesh, in_specs=placed, out_specs=P(("seq", "ctx"), None), check_vma=False
    )
```

profile of v0, /device:TPU:6, one launch (start us, length us, event | category | flops | bytes accessed | tf_op | source)
XLA Modules:
  0.0 881.0 jit_solution(1042140750232295517)
XLA Ops:
  6.5 1.8 copy.67
  8.4 0.7 all-gather.3.cloned.1.call-update
  9.1 0.8 copy.72
  10.2 0.7 add_reduce_fusion
  10.9 1.3 copy.68
  12.2 1.0 copy.70
  13.2 0.7 convert_element_type.75
  13.9 0.6 reduce-window.6
  14.5 0.2 slice_reduce_fusion
  15.1 0.2 min.11
  15.3 0.7 compare_select_fusion
  16.4 96.0 %all-gather.5.cloned.1.call-done = bf16[4096,512]{0,1:T(8,128)(2,1)} async-done(((bf16[128,512]{0,1:T(8,128)(2,1)}), bf16[4096,512]{0,1:T(8,128)(2,1)}) %all-gather.5.cloned.1.call-update) | async-done | bytes 4194320 | tf_op jit(solution)/shard_map/all_gather | solution.py:68
  112.3 6.3 copy.69
  118.7 87.7 %all-gather.3.cloned.1.call-done = bf16[4096,512]{1,0:T(8,128)(2,1)} async-done(((bf16[128,512]{1,0:T(8,128)(2,1)}), bf16[4096,512]{1,0:T(8,128)(2,1)}) %all-gather.3.cloned.1.call-update) | async-done | bytes 4194320 | tf_op jit(solution)/shard_map/all_gather | solution.py:69
  206.4 6.5 copy.66
  213.0 42.7 %while.16 = (s32[]{:T(128)}, f32[128,4,4,128]{0,3,2,1:T(8,128)S(1)}, f32[4,4,128]{2,1,0:T(4,128)S(1)}, s32[]{:T(128)}, bf16[4096,4,128]{0,2,1:T(8,128)(2,1)}, /*...) while((s32[]{:T(128)}, ...), condition=%wide.region_5.6_spmd.clone, body=%wide.region_1.5_spmd.clone.sunk | while | flops 545587840 | bytes 12294425 | solution.py:77
  213.7 5.3 conditional.3
  213.9 2.5 fusion.2
  216.4 2.5 fusion.10
  219.7 5.3 conditional.3
  219.8 2.5 fusion.2
  222.4 2.5 fusion.10
  225.7 5.3 conditional.3
  225.8 2.5 fusion.2
  228.4 2.5 fusion.10
  231.6 5.3 conditional.3
  231.8 2.5 fusion.2
  234.4 2.5 fusion.10
  237.6 5.3 conditional.3
  237.8 2.5 fusion.2
  240.4 2.5 fusion.10
  243.6 5.3 conditional.3
  243.8 2.5 fusion.2
  246.4 2.5 fusion.10
  249.6 5.3 conditional.3
  249.8 2.5 fusion.2
  252.4 2.5 fusion.10
  255.9 1.3 copy.85
  257.2 1.6 fusion.48
  258.9 0.4 fusion.81
  259.4 66.4 %psum.56 = f32[32]{0:T(128)S(1)} all-reduce(f32[32]{0:T(128)S(1)} %fusion.77), channel_id=1, replica_groups=mesh['seq'=24,'ctx'=32] {'ctx'}, use_global_device_ids=true, to_apply=%region_13.14 | all-reduce | flops 32 | bytes 256 | tf_op jit(solution)/shard_map/psum | solution.py:111
  325.9 0.2 fusion.72
  326.1 70.6 %psum.57 = f32[32]{0:T(128)S(1)} all-reduce(f32[32]{0:T(128)S(1)} %fusion.72), channel_id=1, replica_groups=mesh['seq'=24,'ctx'=32] {'ctx'}, use_global_device_ids=true, to_apply=%region_16.17 | all-reduce | flops 32 | bytes 256 | tf_op jit(solution)/shard_map/psum | solution.py:111
  396.8 0.2 fusion.80
  397.0 73.0 %psum.58 = f32[32]{0:T(128)S(1)} all-reduce(f32[32]{0:T(128)S(1)} %get-tuple-element.254), channel_id=1, replica_groups=mesh['seq'=24,'ctx'=32] {'ctx'}, use_global_device_ids=true, to_apply=%region_19.20 | all-reduce | flops 32 | bytes 256 | tf_op jit(solution)/shard_map/psum | solution.py:111
  470.0 1.5 fusion.23
  471.5 16.7 %all-to-all-start = ((bf16[32,1,8,2048]{3,2,1,0:T(8,128)(2,1)}), bf16[32,1,8,2048]{3,2,1,0:T(8,128)(2,1)}, u32[]{:S(2)}, u32[]{:S(2)}) async-start(bf16[32,1,8,2048]{3,2,1,0:T(8,128)(2,1)} %fusion.23), calls=%async_computation | async-start | bytes 2097152 | tf_op jit(solution)/shard_map/all_to_all | solution.py:129
  488.3 0.2 fusion.73
  488.5 69.7 %psum.59 = f32[32]{0:T(128)S(1)} all-reduce(f32[32]{0:T(128)S(1)} %fusion.73), channel_id=1, replica_groups=mesh['seq'=24,'ctx'=32] {'ctx'}, use_global_device_ids=true, to_apply=%region_22.23 | all-reduce | flops 32 | bytes 256 | tf_op jit(solution)/shard_map/psum | solution.py:111
  558.3 0.2 fusion.78
  558.5 67.7 %psum.60 = f32[32]{0:T(128)S(1)} all-reduce(f32[32]{0:T(128)S(1)} %fusion.78), channel_id=1, replica_groups=mesh['seq'=24,'ctx'=32] {'ctx'}, use_global_device_ids=true, to_apply=%region_25.26 | all-reduce | flops 32 | bytes 256 | tf_op jit(solution)/shard_map/psum | solution.py:111
  626.3 0.2 fusion.74
  626.5 73.0 %psum.61 = f32[32]{0:T(128)S(1)} all-reduce(f32[32]{0:T(128)S(1)} %fusion.74), channel_id=1, replica_groups=mesh['seq'=24,'ctx'=32] {'ctx'}, use_global_device_ids=true, to_apply=%region_28.29 | all-reduce | flops 32 | bytes 256 | tf_op jit(solution)/shard_map/psum | solution.py:111
  699.5 2.6 fusion.30
  702.2 4.3 fusion.24
  706.5 17.6 %all-to-all-start.1 = ((bf16[32,1,8,2048]{3,2,1,0:T(8,128)(2,1)}), bf16[32,1,8,2048]{3,2,1,0:T(8,128)(2,1)S(1)}, u32[]{:S(2)}, u32[]{:S(2)}) async-start(bf16[32,1,8,2048]{3,2,1,0:T(8,128)(2,1)} %fusion.24), calls=%async_computation.1 | async-start | bytes 2097152 | tf_op jit(solution)/shard_map/all_to_all | solution.py:136
  724.1 0.2 fusion.79
  724.3 69.8 %psum.62 = f32[32]{0:T(128)S(1)} all-reduce(f32[32]{0:T(128)S(1)} %get-tuple-element.252), channel_id=1, replica_groups=mesh['seq'=24,'ctx'=32] {'ctx'}, use_global_device_ids=true, to_apply=%region_31.32 | all-reduce | flops 32 | bytes 256 | tf_op jit(solution)/shard_map/psum | solution.py:111
  794.1 0.2 fusion.75
  794.3 67.9 %psum.63 = f32[32]{0:T(128)S(1)} all-reduce(f32[32]{0:T(128)S(1)} %fusion.75), channel_id=1, replica_groups=mesh['seq'=24,'ctx'=32] {'ctx'}, use_global_device_ids=true, to_apply=%region_34.35 | all-reduce | flops 32 | bytes 256 | tf_op jit(solution)/shard_map/psum | solution.py:111
  862.6 2.3 gather_fusion
  865.0 3.5 reshape.201
  868.4 4.8 multiply_reduce_fusion
  873.2 0.9 fusion.51
  (101 shorter events, 3.8 us)
Async XLA Ops:
  6.5 695.7 %copy-start = (bf16[1,512,2048]{2,1,0:T(8,128)(2,1)S(1)}, bf16[1,512,2048]{2,1,0:T(8,128)(2,1)}, u32[]{:S(2)}) copy-start(bf16[1,512,2048]{2,1,0:T(8,128)(2,1)} %param.22) | copy-start | bytes 6291460
  6.5 105.8 %all-gather.5.cloned.1.call-start = ((), (), s32[]{:S(2)}) async-start(), calls=%async_computation.3 | async-start | bytes 4325376 | tf_op jit(solution)/shard_map/all_gather | solution.py:68
  8.4 198.0 %all-gather.3.cloned.1.call-start = ((), (), s32[]{:S(2)}) async-start(), calls=%async_computation.2 | async-start | bytes 4325376 | tf_op jit(solution)/shard_map/all_gather | solution.py:69
  255.7 3.2 copy-start.4
  258.8 443.3 %copy-start.1 = (bf16[128,2048]{1,0:T(8,128)(2,1)}, bf16[128,2048]{1,0:T(8,128)(2,1)S(1)}, u32[]{:S(2)}) copy-start(bf16[128,2048]{1,0:T(8,128)(2,1)S(1)} %get-tuple-element.259) | copy-start | bytes 1572868
  471.5 228.0 %all-to-all-start = ((bf16[32,1,8,2048]{3,2,1,0:T(8,128)(2,1)}), bf16[32,1,8,2048]{3,2,1,0:T(8,128)(2,1)}, u32[]{:S(2)}, u32[]{:S(2)}) async-start(bf16[32,1,8,2048]{3,2,1,0:T(8,128)(2,1)} %fusion.23), calls=%async_computation | async-start | bytes 2097152 | tf_op jit(solution)/shard_map/all_to_all | solution.py:129
  702.2 160.2 %copy-start.3 = (s32[128,2]{0,1:T(2,128)S(1)}, s32[128,2]{0,1:T(2,128)}, u32[]{:S(2)}) copy-start(s32[128,2]{0,1:T(2,128)} %param.23) | copy-start | bytes 3076
  706.5 156.1 %all-to-all-start.1 = ((bf16[32,1,8,2048]{3,2,1,0:T(8,128)(2,1)}), bf16[32,1,8,2048]{3,2,1,0:T(8,128)(2,1)S(1)}, u32[]{:S(2)}, u32[]{:S(2)}) async-start(bf16[32,1,8,2048]{3,2,1,0:T(8,128)(2,1)} %fusion.24), calls=%async_computation.1 | async-start | bytes 2097152 | tf_op jit(solution)/shard_map/all_to_all | solution.py:136
  865.0 8.3 copy-start.2
Sparse Core Ops, SparseCore 0:
  11.0 101.2 all-gather.4
  116.1 90.2 all-gather.2
where the time goes:
time: 895 us; the launch traced here: 881 us
  blocking collectives  558 us (62%)
  waiting for transfers between devices  184 us (21%)
  matrix products  44.4 us (5%)
  starting transfers between devices  34.3 us (4%)
  local copies, waits for them, and re-layouts  26.3 us (3%)
  other arithmetic  13.9 us (2%)
  between operations  13.7 us (2%)
    psum x8, blocking collectives, per_device(): columns = lax.psum(jnp.sum(plan, 0), 'ctx')  558 us
    all_gather x1, waiting for transfers between devices, attend(): key_piece = lax.all_gather(keys, 'ctx', axis=0, tiled=True)  96 us
    all_gather x1, waiting for transfers between devices, attend(): value_piece = lax.all_gather(values, 'ctx', axis=0, tiled=True)  87.7 us
  transfers between devices with their start and end apart: 4, of which 2 were waited for; matrix products, arithmetic and copies ran while one was open for 2% of the time, Pallas kernels for 0%

commit v1 on v0

--- a/solution.py
+++ b/solution.py
@@ -3,6 +3,8 @@
 import jax
 import jax.numpy as jnp
 from jax import lax
+from jax.experimental import pallas as pl
+from jax.experimental.pallas import tpu as pltpu
 from jax.sharding import PartitionSpec as P
 
 HEADS = 16
@@ -83,62 +85,293 @@
     return results
 
 
+MESH = pl.DeviceIdType.MESH
+NX = 4
+NY = 8
+PEERS = NX * NY
+SLOTS = 8
+VMEM_LIMIT = 56 * 1024 * 1024
+
+
+def shifted(me, dx, dy):
+    return lax.rem(me // NY + dx + NX, NX) * NY + lax.rem(lax.rem(me, NY) + dy + NY, NY)
+
+
+def moe_kernel(
+    tokens,
+    attended,
+    gain,
+    router,
+    picks,
+    w_gate,
+    w_up,
+    w_down,
+    layer,
+    gate_w,
+    up_w,
+    down_w,
+    resid,
+    outbox,
+    inbox,
+    results,
+    returns,
+    plans,
+    weight_sem,
+    plan_send,
+    plan_recv,
+    out_send,
+    out_recv,
+    back_send,
+    back_recv,
+):
+    me = lax.axis_index("ctx")
+    rows, width = tokens.shape
+    experts = router.shape[1]
+
+    def to_peer(k):
+        return shifted(me, k // NY, lax.rem(k, NY))
+
+    def from_peer(k):
+        return shifted(me, -(k // NY), -lax.rem(k, NY))
+
+    barrier = pltpu.get_barrier_semaphore()
+
+    @pl.loop(1, PEERS)
+    def _(k):
+        pl.semaphore_signal(barrier, inc=1, device_id={"ctx": to_peer(k)}, device_id_type=MESH)
+
+    loads = [
+        pltpu.make_async_copy(src, dst, weight_sem.at[i])
+        for i, (src, dst) in enumerate(((w_gate, gate_w), (w_up, up_w), (w_down, down_w)))
+    ]
+    for load in loads:
+        load.start()
+
+    stream = (tokens[...].astype(jnp.float32) + attended[...].astype(jnp.float32)).astype(
+        jnp.bfloat16
+    )
+    resid[...] = stream
+    stream = stream.astype(jnp.float32)
+    mean_square = jnp.mean(stream * stream, -1, keepdims=True)
+    normed = (stream * lax.rsqrt(mean_square + epsilon) * gain[...].astype(jnp.float32)).astype(
+        jnp.bfloat16
+    )
+    logits = logit_cap * jnp.tanh(
+        jnp.dot(normed, router[...], preferred_element_type=jnp.float32) / logit_cap
+    )
+    plan = jnp.exp(logits.T)
+    plan = plan / jnp.sum(plan, 0, keepdims=True)
+    plans[0] = plan.astype(jnp.bfloat16)
+
+    pl.semaphore_wait(barrier, PEERS - 1)
+
+    def plan_column(dy):
+        return pltpu.make_async_remote_copy(
+            src_ref=plans.at[0],
+            dst_ref=plans.at[dy],
+            send_sem=plan_send.at[dy],
+            recv_sem=plan_recv.at[dy],
+            device_id={"ctx": shifted(me, 0, dy)},
+            device_id_type=MESH,
+        )
+
+    def plan_row(dx):
+        return pltpu.make_async_remote_copy(
+            src_ref=plans.at[pl.ds(0, NY)],
+            dst_ref=plans.at[pl.ds(dx * NY, NY)],
+            send_sem=plan_send.at[NY + dx],
+            recv_sem=plan_recv.at[NY + dx],
+            device_id={"ctx": shifted(me, dx, 0)},
+            device_id_type=MESH,
+        )
+
+    for dy in range(1, NY):
+        plan_column(dy).start()
+
+    picked = picks[...]
+    offset = lax.rem(picked // NY - me // NY + NX, NX) * NY + lax.rem(
+        lax.rem(picked, NY) - lax.rem(me, NY) + NY, NY
+    )
+    number = lax.broadcasted_iota(jnp.int32, (PEERS, rows), 0)
+    chosen = [number == offset[j : j + 1] for j in range(2)]
+    either = jnp.where(chosen[0] | chosen[1], 1.0, 0.0)
+    earlier = jnp.where(
+        lax.broadcasted_iota(jnp.int32, (rows, rows), 0)
+        < lax.broadcasted_iota(jnp.int32, (rows, rows), 1),
+        1.0,
+        0.0,
+    ).astype(jnp.bfloat16)
+    ranks = jnp.dot(either.astype(jnp.bfloat16), earlier, preferred_element_type=jnp.float32)
+    place = jnp.where(either > 0.0, ranks, -1.0)
+    slot = lax.broadcasted_iota(jnp.int32, (PEERS, SLOTS, rows), 1).astype(jnp.float32)
+    held = jnp.where(place[:, None, :] == slot, 1.0, 0.0).reshape(PEERS * SLOTS, rows)
+    packed = jnp.dot(held.astype(jnp.bfloat16), normed, preferred_element_type=jnp.float32)
+    packed = packed.astype(jnp.bfloat16).reshape(PEERS, SLOTS, width)
+    outbox[...] = packed
+
+    def outward(k):
+        return pltpu.make_async_remote_copy(
+            src_ref=outbox.at[k],
+            dst_ref=inbox.at[k],
+            send_sem=out_send.at[k],
+            recv_sem=out_recv.at[k],
+            device_id={"ctx": to_peer(k)},
+            device_id_type=MESH,
+        )
+
+    def backward(k):
+        return pltpu.make_async_remote_copy(
+            src_ref=results.at[k],
+            dst_ref=returns.at[k],
+            send_sem=back_send.at[k],
+            recv_sem=back_recv.at[k],
+            device_id={"ctx": from_peer(k)},
+            device_id_type=MESH,
+        )
+
+    @pl.loop(1, PEERS)
+    def _(k):
+        outward(k).start()
+
+    inbox[0] = outbox[0]
+
+    for dy in range(1, NY):
+        plan_column(dy).wait_recv()
+    for dx in range(1, NX):
+        plan_row(dx).start()
+
+    for load in loads:
+        load.wait()
+
+    @pl.loop(0, NX)
+    def _(chunk):
+        first = chunk * NY
+
+        @pl.loop(jnp.maximum(first, 1), first + NY)
+        def _(k):
+            outward(k).wait_recv()
+
+        block = inbox[pl.ds(first, NY)].reshape(NY * SLOTS, width)
+        gate = jnp.dot(block, gate_w[...], preferred_element_type=jnp.float32)
+        upward = jnp.dot(block, up_w[...], preferred_element_type=jnp.float32)
+        hidden = (gate / (1.0 + jnp.exp(-gate)) * upward).astype(jnp.bfloat16)
+        given = jnp.dot(hidden, down_w[...], preferred_element_type=jnp.float32)
+        results[pl.ds(first, NY)] = given.astype(jnp.bfloat16).reshape(NY, SLOTS, width)
+
+        @pl.loop(jnp.maximum(first, 1), first + NY)
+        def _(k):
+            backward(k).start()
+
+    returns[0] = results[0]
+
+    for dx in range(1, NX):
+        plan_row(dx).wait_recv()
+
+    target = float(rows * PEERS * 2 / experts)
+
+    def column_sums(scale):
+        def add(s, total):
+            block = plans[s].astype(jnp.float32)
+            if scale is None:
+                return total + block
+            return total + block * (2.0 / jnp.sum(block * scale, 0, keepdims=True))
+
+        total = lax.fori_loop(0, PEERS, add, jnp.zeros((experts, rows), jnp.float32), unroll=4)
+        return jnp.sum(total, 1, keepdims=True)
+
+    scale = target / column_sums(None)
+    scale = lax.fori_loop(0, ITERS - 1, lambda _, s: target / column_sums(s), scale)
+    plan = plan * scale
+    plan = plan * (2.0 / jnp.sum(plan, 0, keepdims=True))
+    named = lax.broadcasted_iota(jnp.int32, (experts, rows), 0)
+    mass = [
+        jnp.sum(jnp.where(named == picked[j : j + 1], plan, 0.0), 0, keepdims=True)
+        for j in range(2)
+    ]
+    total = mass[0] + mass[1]
+    gates = jnp.where(chosen[0], mass[0] / total, 0.0) + jnp.where(chosen[1], mass[1] / total, 0.0)
+    mixing = jnp.where(place[:, None, :] == slot, gates[:, None, :], 0.0)
+    mixing = mixing.reshape(PEERS * SLOTS, rows).T
+    high = mixing.astype(jnp.bfloat16)
+    low = (mixing - high.astype(jnp.float32)).astype(jnp.bfloat16)
+
+    @pl.loop(1, PEERS)
+    def _(k):
+        backward(k).wait_recv()
+
+    step = 512
+    for first in range(0, width, step):
+        columns = pl.ds(first, step)
+        block = returns[:, :, columns].reshape(PEERS * SLOTS, step)
+        mixture = jnp.dot(high, block, preferred_element_type=jnp.float32) + jnp.dot(
+            low, block, preferred_element_type=jnp.float32
+        )
+        layer[:, columns] = (resid[:, columns].astype(jnp.float32) + mixture).astype(jnp.bfloat16)
+
+    @pl.loop(1, PEERS)
+    def _(k):
+        outward(k).wait_send()
+        backward(k).wait_send()
+
+    for dy in range(1, NY):
+        plan_column(dy).wait_send()
+    for dx in range(1, NX):
+        plan_row(dx).wait_send()
+
+
+def experts_of(tokens, attended, norm_gain, router, w_gate, w_up, w_down, picks):
+    rows, width = tokens.shape
+    hidden = w_gate.shape[-1]
+    experts = router.shape[1]
+    whole = pl.BlockSpec(memory_space=pltpu.VMEM)
+    apart = pl.BlockSpec(memory_space=pl.ANY)
+    box = pltpu.VMEM((PEERS, SLOTS, width), jnp.bfloat16)
+    sems = pltpu.SemaphoreType.DMA
+    return pl.pallas_call(
+        moe_kernel,
+        out_shape=jax.ShapeDtypeStruct((rows, width), jnp.bfloat16),
+        in_specs=[whole] * 5 + [apart] * 3,
+        out_specs=whole,
+        scratch_shapes=[
+            pltpu.VMEM((width, hidden), jnp.bfloat16),
+            pltpu.VMEM((width, hidden), jnp.bfloat16),
+            pltpu.VMEM((hidden, width), jnp.bfloat16),
+            pltpu.VMEM((rows, width), jnp.bfloat16),
+            box,
+            box,
+            box,
+            box,
+            pltpu.VMEM((PEERS, experts, rows), jnp.bfloat16),
+            sems((3,)),
+            sems((NY + NX,)),
+            sems((NY + NX,)),
+            sems((PEERS,)),
+            sems((PEERS,)),
+            sems((PEERS,)),
+            sems((PEERS,)),
+        ],
+        compiler_params=pltpu.CompilerParams(
+            collective_id=1, has_side_effects=True, vmem_limit_bytes=VMEM_LIMIT
+        ),
+        name="experts",
+    )(
+        tokens,
+        attended,
+        norm_gain.reshape(1, width),
+        router,
+        picks.T,
+        w_gate[0],
+        w_up[0],
+        w_down[0],
+    )
+
+
 def per_device(tokens, queries, keys, values, norm_gain, router, w_gate, w_up, w_down, picks):
-    devices = lax.axis_size("ctx")
     my_index = lax.axis_index("ctx")
     my_rows = tokens.shape[0]
     offsets = jnp.arange(my_rows, dtype=jnp.int32) + my_index * my_rows
     attended = attend([(queries, offsets)], keys, values)[0]
-    stream = (
-        (tokens.astype(jnp.float32) + attended.astype(jnp.float32))
-        .astype(jnp.bfloat16)
-        .astype(jnp.float32)
-    )
-    mean_square = jnp.mean(stream * stream, -1, keepdims=True)
-    normed = (stream * lax.rsqrt(mean_square + epsilon) * norm_gain.astype(jnp.float32)).astype(
-        jnp.bfloat16
-    )
-    logits = logit_cap * jnp.tanh(
-        jnp.dot(normed, router, preferred_element_type=jnp.float32) / logit_cap
-    )
-    plan = jnp.exp(logits)
-    plan = plan / jnp.sum(plan, -1, keepdims=True)
-    experts = router.shape[1]
-    top_count = picks.shape[1]
-    capacity = max(2, my_rows * top_count // experts)
-    target = my_rows * devices * top_count / experts
-    for sweep in range(ITERS):
-        columns = lax.psum(jnp.sum(plan, 0), "ctx")
-        plan = plan * (target / columns)
-        plan = plan * (top_count / jnp.sum(plan, -1, keepdims=True))
-    chooses = picks[:, :, None] == jnp.arange(experts, dtype=jnp.int32)[None, None, :]
-    chosen = jnp.sum(jnp.where(chooses, plan[:, None, :], 0.0), -1)
-    gates = chosen / jnp.sum(chosen, -1, keepdims=True)
-    flags = chooses.reshape(my_rows * top_count, experts).astype(jnp.int32)
-    ranks = jnp.cumsum(flags, 0) - flags
-    slots = jnp.sum(ranks * flags, -1).reshape(my_rows, top_count)
-    kept = slots < capacity
-    targets = picks * capacity + jnp.minimum(slots, capacity - 1)
-    slot_ids = jnp.arange(experts * capacity, dtype=jnp.int32)
-    selected = jnp.any(
-        (slot_ids[:, None, None] == targets[None, :, :]) & kept[None, :, :], -1
-    ).astype(jnp.bfloat16)
-    outgoing = jnp.dot(selected, normed, preferred_element_type=jnp.float32).astype(jnp.bfloat16)
-    local_experts = w_gate.shape[0]
-    outgoing = outgoing.reshape(devices, local_experts, capacity, normed.shape[1])
-    incoming = lax.all_to_all(outgoing, "ctx", split_axis=0, concat_axis=0, tiled=True)
-    gate = jnp.einsum("secd,edf->secf", incoming, w_gate, preferred_element_type=jnp.float32)
-    upward = jnp.einsum("secd,edf->secf", incoming, w_up, preferred_element_type=jnp.float32)
-    hidden = (jax.nn.silu(gate) * upward).astype(jnp.bfloat16)
-    processed = jnp.einsum(
-        "secf,efd->secd", hidden, w_down, preferred_element_type=jnp.float32
-    ).astype(jnp.bfloat16)
-    back_rows = lax.all_to_all(processed, "ctx", split_axis=0, concat_axis=0, tiled=True)
-    flat_back = back_rows.reshape(experts * capacity, normed.shape[1])
-    gathered = flat_back[targets]
-    scale = jnp.where(kept, gates, 0.0)
-    mixture = jnp.sum(gathered.astype(jnp.float32) * scale[:, :, None], 1)
-    return (stream + mixture).astype(jnp.bfloat16)
+    return experts_of(tokens, attended, norm_gain, router, w_gate, w_up, w_down, picks)
 
 
 def solution(mesh):

time: 895 us -> 326 us (0.36); the launches traced: 881 us -> 323 us
  blocking collectives: 558 us -> 0 us
  Pallas kernels: 0 us -> 59.5 us
  starting transfers between devices: 34.3 us -> 0.04 us
  other arithmetic: 13.9 us -> 1.85 us
  matrix products: 44.4 us -> 34.2 us
    psum x8 -> x0, blocking collectives: 558 us -> none  [per_device(): columns = lax.psum(jnp.sum(plan, 0), 'ctx')]
    pallas_call x0 -> x1, Pallas kernels: none -> 59.5 us  [experts_of(): pl.pallas_call(moe_kernel, out_shape=jax.ShapeDtypeStruct((rows, width),...]
    all_to_all x2 -> x0, starting transfers between devices: 34.3 us -> none  [the longest x1 17.6 us: per_device(): lax.all_to_all(processed, 'ctx', split_axis=0, concat_axis=0, tiled=True)]
  transfers between devices with their start and end apart: 4 -> 2, of which waited for: 2 -> 2; matrix products, arithmetic and copies ran while one was open for 2% -> 4% of each run, Pallas kernels for 0% -> 0%
where the time goes in v1:
time: 326 us; the launch traced here: 323 us
  waiting for transfers between devices  186 us (57%)
  Pallas kernels  59.5 us (18%)
  matrix products  34.2 us (10%)
  local copies, waits for them, and re-layouts  22.2 us (7%)
  between operations  13.5 us (4%)
  loops' own time  5.17 us (2%)
    all_gather x1, waiting for transfers between devices, attend(): key_piece = lax.all_gather(keys, 'ctx', axis=0, tiled=True)  97.9 us
    all_gather x1, waiting for transfers between devices, attend(): value_piece = lax.all_gather(values, 'ctx', axis=0, tiled=True)  87.8 us
    pallas_call x1, Pallas kernels, experts_of(): pl.pallas_call(moe_kernel, out_shape=jax.ShapeDtypeStruct((rows, width),...  59.5 us
    dot_general x7, matrix products, compute(): jnp.einsum('kgtr,rkd->tkgd', weights.astype(jnp.bfloat16), value_block, p...  17.6 us
    dot_general x7, matrix products, compute(): jnp.einsum('tkgd,rkd->kgtr', query_heads, key_block, preferred_element_ty...  16.5 us
    unnamed x6, local copies, waits for them, and re-layouts  13.4 us
  transfers between devices with their start and end apart: 2, of which 2 were waited for; matrix products, arithmetic and copies ran while one was open for 4% of the time, Pallas kernels for 0%

profile of v1, /device:TPU:6, one launch (start us, length us, event | category | flops | bytes accessed | tf_op | source)
XLA Modules:
  0.0 322.8 jit_solution(5439422409344741047)
XLA Ops:
  6.5 0.0 all-gather.5.cloned.1.call-start
  6.5 1.7 copy.17
  8.2 0.0 all-gather.5.cloned.1.call-update
  8.2 0.0 all-gather.3.cloned.1.call-start
  8.3 0.7 all-gather.3.cloned.1.call-update
  9.0 0.6 add_reduce_fusion
  9.6 1.3 copy.18
  10.9 0.3 copy.20
  11.2 1.9 copy.22.router
  13.1 1.3 reshape.53.gain
  14.4 97.9 %all-gather.5.cloned.1.call-done = bf16[4096,512]{0,1:T(8,128)(2,1)} async-done(((bf16[128,512]{0,1:T(8,128)(2,1)}), bf16[4096,512]{0,1:T(8,128)(2,1)}) %all-gather.5.cloned.1.call-update) | async-done | bytes 4194320 | tf_op jit(solution)/shard_map/all_gather | solution.py:70
  112.3 6.3 %copy.19 = bf16[4096,4,128]{2,0,1:T(8,128)(2,1)} copy(bf16[4096,4,128]{0,2,1:T(8,128)(2,1)} %bitcast.38) | data formatting | bytes 8388608
  118.6 87.8 %all-gather.3.cloned.1.call-done = bf16[4096,512]{1,0:T(8,128)(2,1)} async-done(((bf16[128,512]{1,0:T(8,128)(2,1)}), bf16[4096,512]{1,0:T(8,128)(2,1)}) %all-gather.3.cloned.1.call-update) | async-done | bytes 4194320 | tf_op jit(solution)/shard_map/all_gather | solution.py:71
  206.4 6.4 %copy.16 = bf16[4096,512]{0,1:T(8,128)(2,1)} copy(bf16[4096,512]{1,0:T(8,128)(2,1)} %all-gather.3.cloned.1.call-done) | data formatting | bytes 8388608 | tf_op jit(solution)/shard_map/all_gather | solution.py:71
  212.8 0.1 broadcast_in_dim.21
  212.9 40.5 %while.16 = (s32[]{:T(128)}, f32[128,4,4,128]{0,3,2,1:T(8,128)S(1)}, f32[4,4,128]{2,1,0:T(4,128)S(1)}, s32[]{:T(128)}, bf16[4096,4,128]{0,2,1:T(8,128)(2,1)}, /*...) while((s32[]{:T(128)}, ...), condition=%wide.region_5.6_spmd.clone, body=%wide.region_1.5_spmd.clone.sunk | while | flops 545587840 | bytes 12294425 | solution.py:79
  213.5 5.1 %conditional.3 = ((f32[128,4,4,128]{0,3,2,1:T(8,128)S(1)}, f32[4,4,128]{2,1,0:T(4,128)S(1)})) conditional(s32[]{:T(128)} %convert_element_type.26, (f32[128,4,4,128]{0,3,2,1:T(8,128)S(1)}, f32[4,4,128]{2,1,0:T(4,128)S(1)}) %tuple.44, (s32[]{:T(128)}, bf16[4096,4,128]{0,2,1:T(8,128)(2,1)}, s32[128]{0:T(128)S(1)}, bf16[4096,4,128]{2,0,1:T(8,128)(2,1)}, ...), branch_computations={%region_2.0_spmd, %region_3.4_spmd} | conditional | flops 545587840 | bytes 12293706 | solution.py:49
  213.5 0.1 broadcast_compare_fusion
  213.7 2.4 fusion.2
  216.0 2.5 fusion.10
  219.2 5.1 %conditional.3 = ((f32[128,4,4,128]{0,3,2,1:T(8,128)S(1)}, f32[4,4,128]{2,1,0:T(4,128)S(1)})) conditional(s32[]{:T(128)} %convert_element_type.26, (f32[128,4,4,128]{0,3,2,1:T(8,128)S(1)}, f32[4,4,128]{2,1,0:T(4,128)S(1)}) %tuple.44, (s32[]{:T(128)}, bf16[4096,4,128]{0,2,1:T(8,128)(2,1)}, s32[128]{0:T(128)S(1)}, bf16[4096,4,128]{2,0,1:T(8,128)(2,1)}, ...), branch_computations={%region_2.0_spmd, %region_3.4_spmd} | conditional | flops 545587840 | bytes 12293706 | solution.py:49
  219.2 0.1 broadcast_compare_fusion
  219.4 2.4 fusion.2
  221.7 2.5 fusion.10
  224.9 5.1 %conditional.3 = ((f32[128,4,4,128]{0,3,2,1:T(8,128)S(1)}, f32[4,4,128]{2,1,0:T(4,128)S(1)})) conditional(s32[]{:T(128)} %convert_element_type.26, (f32[128,4,4,128]{0,3,2,1:T(8,128)S(1)}, f32[4,4,128]{2,1,0:T(4,128)S(1)}) %tuple.44, (s32[]{:T(128)}, bf16[4096,4,128]{0,2,1:T(8,128)(2,1)}, s32[128]{0:T(128)S(1)}, bf16[4096,4,128]{2,0,1:T(8,128)(2,1)}, ...), branch_computations={%region_2.0_spmd, %region_3.4_spmd} | conditional | flops 545587840 | bytes 12293706 | solution.py:49
  224.9 0.1 broadcast_compare_fusion
  225.0 2.4 fusion.2
  227.4 2.5 fusion.10
  230.5 5.1 %conditional.3 = ((f32[128,4,4,128]{0,3,2,1:T(8,128)S(1)}, f32[4,4,128]{2,1,0:T(4,128)S(1)})) conditional(s32[]{:T(128)} %convert_element_type.26, (f32[128,4,4,128]{0,3,2,1:T(8,128)S(1)}, f32[4,4,128]{2,1,0:T(4,128)S(1)}) %tuple.44, (s32[]{:T(128)}, bf16[4096,4,128]{0,2,1:T(8,128)(2,1)}, s32[128]{0:T(128)S(1)}, bf16[4096,4,128]{2,0,1:T(8,128)(2,1)}, ...), branch_computations={%region_2.0_spmd, %region_3.4_spmd} | conditional | flops 545587840 | bytes 12293706 | solution.py:49
  230.6 0.1 broadcast_compare_fusion
  230.7 2.4 fusion.2
  233.1 2.5 fusion.10
  236.2 5.1 %conditional.3 = ((f32[128,4,4,128]{0,3,2,1:T(8,128)S(1)}, f32[4,4,128]{2,1,0:T(4,128)S(1)})) conditional(s32[]{:T(128)} %convert_element_type.26, (f32[128,4,4,128]{0,3,2,1:T(8,128)S(1)}, f32[4,4,128]{2,1,0:T(4,128)S(1)}) %tuple.44, (s32[]{:T(128)}, bf16[4096,4,128]{0,2,1:T(8,128)(2,1)}, s32[128]{0:T(128)S(1)}, bf16[4096,4,128]{2,0,1:T(8,128)(2,1)}, ...), branch_computations={%region_2.0_spmd, %region_3.4_spmd} | conditional | flops 545587840 | bytes 12293706 | solution.py:49
  236.3 0.1 broadcast_compare_fusion
  236.4 2.4 fusion.2
  238.8 2.5 fusion.10
  241.9 5.1 %conditional.3 = ((f32[128,4,4,128]{0,3,2,1:T(8,128)S(1)}, f32[4,4,128]{2,1,0:T(4,128)S(1)})) conditional(s32[]{:T(128)} %convert_element_type.26, (f32[128,4,4,128]{0,3,2,1:T(8,128)S(1)}, f32[4,4,128]{2,1,0:T(4,128)S(1)}) %tuple.44, (s32[]{:T(128)}, bf16[4096,4,128]{0,2,1:T(8,128)(2,1)}, s32[128]{0:T(128)S(1)}, bf16[4096,4,128]{2,0,1:T(8,128)(2,1)}, ...), branch_computations={%region_2.0_spmd, %region_3.4_spmd} | conditional | flops 545587840 | bytes 12293706 | solution.py:49
  242.0 0.1 broadcast_compare_fusion
  242.1 2.4 fusion.2
  244.5 2.5 fusion.10
  247.6 5.1 %conditional.3 = ((f32[128,4,4,128]{0,3,2,1:T(8,128)S(1)}, f32[4,4,128]{2,1,0:T(4,128)S(1)})) conditional(s32[]{:T(128)} %convert_element_type.26, (f32[128,4,4,128]{0,3,2,1:T(8,128)S(1)}, f32[4,4,128]{2,1,0:T(4,128)S(1)}) %tuple.44, (s32[]{:T(128)}, bf16[4096,4,128]{0,2,1:T(8,128)(2,1)}, s32[128]{0:T(128)S(1)}, bf16[4096,4,128]{2,0,1:T(8,128)(2,1)}, ...), branch_computations={%region_2.0_spmd, %region_3.4_spmd} | conditional | flops 545587840 | bytes 12293706 | solution.py:49
  247.7 0.1 broadcast_compare_fusion
  247.8 2.4 fusion.2
  250.2 2.5 fusion.10
  253.3 0.1 divide_convert_fusion
  253.5 1.0 copy.26.attended
  254.5 59.5 %experts.1 = bf16[128,2048]{1,0:T(8,128)(2,1)} custom-call(bf16[128,2048]{1,0:T(8,128)(2,1)} %tokens.1, bf16[128,2048]{1,0:T(8,128)(2,1)} %copy.26.attended, bf16[1,2048]{1,0:T(2,128)(2,1)} %reshape.53.gain, bf16[2048,32]{1,0:T(8,128)(2,1)} %copy.22.router, s32[2,128]{1,0:T(2,128)} %bitcast.45, bf16[2048,512]{1,0:T(8,128)(2,1)} %bitcast.39, ...), custom_call_target="tpu_custom_call" | custom-call | tf_op jit(solution)/shard_map/experts/pallas_call | solution.py:330
  314.0 1.9 copy.43
  (31 shorter events, 0.2 us)
Async XLA Ops:
  6.5 105.8 %all-gather.5.cloned.1.call-start = ((), (), s32[]{:S(2)}) async-start(), calls=%async_computation.1 | async-start | bytes 4325376 | tf_op jit(solution)/shard_map/all_gather | solution.py:70
  8.2 198.2 %all-gather.3.cloned.1.call-start = ((), (), s32[]{:S(2)}) async-start(), calls=%async_computation | async-start | bytes 4325376 | tf_op jit(solution)/shard_map/all_gather | solution.py:71
Sparse Core Ops, SparseCore 0:
  11.0 101.2 all-gather.4
  116.1 90.2 all-gather.2

commit v2 on v1

v2 whole, which is shorter than its diff:
```python
import math

import jax
import jax.numpy as jnp
from jax import lax
from jax.experimental import pallas as pl
from jax.experimental.pallas import tpu as pltpu
from jax.sharding import PartitionSpec as P

HEADS = 16
KV_HEADS = 4
GROUP = HEADS // KV_HEADS
HEAD_DIM = 128
ITERS = 8
MESH = pl.DeviceIdType.MESH
NX = 4
NY = 8
PEERS = NX * NY
SLOTS = 8
VMEM_LIMIT = 48 * 1024 * 1024


score_cap = 50.0
logit_cap = 10.0
epsilon = 1e-06


def shifted(me, dx, dy):
    return lax.rem(me // NY + dx + NX, NX) * NY + lax.rem(lax.rem(me, NY) + dy + NY, NY)


def contract_last(left, right):
    return lax.dot_general(
        left, right, (((1,), (1,)), ((), ())), preferred_element_type=jnp.float32
    )


def layer_kernel(
    tokens,
    gain,
    router,
    picks,
    queries,
    keys,
    values,
    w_gate,
    w_up,
    w_down,
    layer,
    gate_w,
    up_w,
    down_w,
    query_rows,
    pairs,
    summed,
    denoms,
    finished,
    attended,
    resid,
    held,
    outbox,
    inbox,
    results,
    returns,
    plans,
    weight_sem,
    own_sem,
    head_send,
    head_recv,
    ring_send,
    ring_recv,
    done_send,
    done_recv,
    plan_send,
    plan_recv,
    out_send,
    out_recv,
    back_send,
    back_recv,
):
    me = lax.axis_index("ctx")
    my_x = me // NY
    my_y = lax.rem(me, NY)
    rows, width = tokens.shape
    experts = router.shape[0]
    group_width = GROUP * HEAD_DIM

    def to_peer(k):
        return shifted(me, k // NY, lax.rem(k, NY))

    def from_peer(k):
        return shifted(me, -(k // NY), -lax.rem(k, NY))

    barrier = pltpu.get_barrier_semaphore()

    @pl.loop(1, PEERS)
    def _(k):
        pl.semaphore_signal(barrier, inc=1, device_id={"ctx": to_peer(k)}, device_id_type=MESH)

    def head_columns(head):
        return pl.ds(pl.multiple_of(head * HEAD_DIM, HEAD_DIM), HEAD_DIM)

    def group_columns(head):
        return pl.ds(pl.multiple_of(head * group_width, group_width), group_width)

    own = [
        (keys.at[:, head_columns(my_x)], pairs.at[my_x, 0, 0]),
        (values.at[:, head_columns(my_x)], pairs.at[my_x, 0, 1]),
        (queries.at[:, group_columns(my_x)], query_rows.at[my_x]),
    ]
    own = [pltpu.make_async_copy(src, dst, own_sem.at[i]) for i, (src, dst) in enumerate(own)]
    for copy in own:
        copy.start()
    loads = [
        pltpu.make_async_copy(src, dst, weight_sem.at[i])
        for i, (src, dst) in enumerate(((w_gate, gate_w), (w_up, up_w), (w_down, down_w)))
    ]
    for load in loads:
        load.start()

    def to_head(dx, part):
        head = lax.rem(my_x + dx, NX)
        if part == 2:
            src, dst = queries.at[:, group_columns(head)], query_rows.at[my_x]
        else:
            src = (keys, values)[part].at[:, head_columns(head)]
            dst = pairs.at[my_x, 0, part]
        return pltpu.make_async_remote_copy(
            src_ref=src,
            dst_ref=dst,
            send_sem=head_send.at[dx, part],
            recv_sem=head_recv.at[dx, part],
            device_id={"ctx": shifted(me, dx, 0)},
            device_id_type=MESH,
        )

    def from_head(dx, part):
        source = lax.rem(my_x - dx + NX, NX)
        dst = query_rows.at[source] if part == 2 else pairs.at[source, 0, part]
        return pltpu.make_async_remote_copy(
            src_ref=dst,
            dst_ref=dst,
            send_sem=head_send.at[dx, part],
            recv_sem=head_recv.at[dx, part],
            device_id={"ctx": shifted(me, dx, 0)},
            device_id_type=MESH,
        )

    pl.semaphore_wait(barrier, PEERS - 1)
    for part in range(3):
        for dx in range(1, NX):
            to_head(dx, part).start()

    picked = picks[...]
    offset = lax.rem(picked // NY - my_x + NX, NX) * NY + lax.rem(
        lax.rem(picked, NY) - my_y + NY, NY
    )
    number = lax.broadcasted_iota(jnp.int32, (PEERS, rows), 0)
    chosen = [number == offset[j : j + 1] for j in range(2)]
    either = jnp.where(chosen[0] | chosen[1], 1.0, 0.0)
    earlier = jnp.where(
        lax.broadcasted_iota(jnp.int32, (rows, rows), 0)
        < lax.broadcasted_iota(jnp.int32, (rows, rows), 1),
        1.0,
        0.0,
    ).astype(jnp.bfloat16)
    ranks = jnp.dot(either.astype(jnp.bfloat16), earlier, preferred_element_type=jnp.float32)
    place = jnp.where(either > 0.0, ranks, -1.0)
    slot = lax.broadcasted_iota(jnp.int32, (PEERS, SLOTS, rows), 1).astype(jnp.float32)
    rows_held = jnp.where(place[:, None, :] == slot, 1.0, 0.0).reshape(PEERS * SLOTS, rows)
    held[...] = rows_held.astype(jnp.bfloat16)

    summed[...] = jnp.zeros_like(summed)
    denoms[...] = jnp.zeros_like(denoms)

    def behind(step):
        return lax.select(step == 0, 0, 2 * step - 1)

    def ahead(step):
        return lax.select(step == 4, 7, 2 * step)

    def ring(up, step, i):
        block = lax.rem(my_x - i + NX, NX)
        place_of = behind if up else ahead
        way = 0 if up else 1
        return pltpu.make_async_remote_copy(
            src_ref=pairs.at[block, place_of(step - 1)],
            dst_ref=pairs.at[block, place_of(step)],
            send_sem=ring_send.at[way, step, i],
            recv_sem=ring_recv.at[way, step, i],
            device_id={"ctx": shifted(me, 0, 1 if up else -1)},
            device_id_type=MESH,
        )

    def forward(step, i):
        step = jnp.int32(step)

        @pl.when((step < 3) | (i < 2))
        def _():
            ring(True, step + 1, i).start()

        @pl.when((step < 3) | (i >= 2))
        def _():
            ring(False, step + 1, i).start()

    def attend(q_block, key_block, value_block, diagonal=False):
        block = query_rows[q_block]
        query = jnp.concatenate(
            [block[:, h * HEAD_DIM : (h + 1) * HEAD_DIM] for h in range(GROUP)], 0
        )
        scores = contract_last(query, key_block)
        weights = jnp.exp2(
            jnp.tanh(scores * (1.0 / (score_cap * math.sqrt(HEAD_DIM))))
            * (score_cap * math.log2(math.e))
        )
        if diagonal:
            row = lax.broadcasted_iota(jnp.int32, (GROUP, rows, rows), 1)
            column = lax.broadcasted_iota(jnp.int32, (GROUP, rows, rows), 2)
            visible = (column <= row).reshape(GROUP * rows, rows)
            weights = jnp.where(visible, weights, 0.0)
        part = weights[:, :rows]
        for first in range(rows, weights.shape[1], rows):
            part = part + weights[:, first : first + rows]
        denoms[q_block] += part
        summed[q_block] += jnp.dot(
            weights.astype(jnp.bfloat16), value_block, preferred_element_type=jnp.float32
        )

    def unit(block, where):
        return pairs[block, where, 0], pairs[block, where, 1]

    def attend_own(i):
        block = lax.rem(my_x - i + NX, NX)
        own_keys, own_values = unit(block, 0)
        attend(block, own_keys, own_values, diagonal=True)

        @pl.loop(block + 1, NX)
        def _(q_block):
            attend(q_block, own_keys, own_values)

    def attend_two(step, i):
        block = lax.rem(my_x - i + NX, NX)

        @pl.when(my_y >= step)
        def _():
            attend(block, *unit(block, 2 * step - 1))

        @pl.when(my_y >= NY - step)
        def _():
            attend(block, *unit(block, 2 * step))

        @pl.loop(block + 1, NX)
        def _(q_block):
            first, second = unit(block, 2 * step - 1), unit(block, 2 * step)
            attend(
                q_block,
                jnp.concatenate([first[0], second[0]], 0),
                jnp.concatenate([first[1], second[1]], 0),
            )

    def attend_opposite(i):
        block = lax.rem(my_x - i + NX, NX)

        @pl.when(my_y >= NY // 2)
        def _():
            attend(block, *unit(block, 7))

        @pl.loop(block + 1, NX)
        def _(q_block):
            attend(q_block, *unit(block, 7))

    for copy in own[:2]:
        copy.wait()
    forward(0, 0)
    for dx in range(1, NX):
        from_head(dx, 0).wait_recv()
        from_head(dx, 1).wait_recv()
        forward(0, dx)
    own[2].wait()
    for dx in range(1, NX):
        from_head(dx, 2).wait_recv()

    def arrive(step, i):
        ring(True, step, i).wait_recv()
        ring(False, step, i).wait_recv()
        forward(step, i)

    @pl.loop(0, NX)
    def _(i):
        arrive(jnp.int32(1), i)
        attend_own(i)

    @pl.loop(2, 4)
    def _(step):
        @pl.loop(0, NX)
        def _(i):
            arrive(step, i)
            attend_two(step - 1, i)

    @pl.loop(0, NX)
    def _(i):
        attend_two(3, i)

        @pl.when(i < 2)
        def _():
            ring(True, jnp.int32(4), i).wait_recv()

        @pl.when(i >= 2)
        def _():
            ring(False, jnp.int32(4), i).wait_recv()

        attend_opposite(i)

    def give(dx):
        block = lax.rem(my_x + dx, NX)
        return pltpu.make_async_remote_copy(
            src_ref=finished.at[block],
            dst_ref=attended.at[my_x],
            send_sem=done_send.at[dx],
            recv_sem=done_recv.at[dx],
            device_id={"ctx": shifted(me, dx, 0)},
            device_id_type=MESH,
        )

    def take(dx):
        source = lax.rem(my_x - dx + NX, NX)
        return pltpu.make_async_remote_copy(
            src_ref=attended.at[source],
            dst_ref=attended.at[source],
            send_sem=done_send.at[dx],
            recv_sem=done_recv.at[dx],
            device_id={"ctx": shifted(me, dx, 0)},
            device_id_type=MESH,
        )

    def normal(block):
        denom = jnp.sum(denoms[block], -1, keepdims=True)
        return (summed[block] / denom).astype(jnp.bfloat16).reshape(GROUP, rows, HEAD_DIM)

    @pl.loop(1, NX)
    def _(dx):
        block = lax.rem(my_x + dx, NX)
        finished[block] = normal(block)
        give(dx).start()

    attended[my_x] = normal(my_x)

    @pl.loop(1, NX)
    def _(dx):
        take(dx).wait_recv()

    square = jnp.zeros((rows, HEAD_DIM), jnp.float32)
    for h in range(HEADS):
        columns = slice(h * HEAD_DIM, (h + 1) * HEAD_DIM)
        stream = (
            tokens[:, columns].astype(jnp.float32)
            + attended[h // GROUP, h % GROUP].astype(jnp.float32)
        ).astype(jnp.bfloat16)
        resid[:, columns] = stream
        stream = stream.astype(jnp.float32)
        square = square + stream * stream
    mean_square = jnp.sum(square, -1, keepdims=True) / width
    normed = (
        resid[...].astype(jnp.float32)
        * lax.rsqrt(mean_square + epsilon)
        * gain[...].astype(jnp.float32)
    ).astype(jnp.bfloat16)

    def outward(k):
        return pltpu.make_async_remote_copy(
            src_ref=outbox.at[k],
            dst_ref=inbox.at[k],
            send_sem=out_send.at[k],
            recv_sem=out_recv.at[k],
            device_id={"ctx": to_peer(k)},
            device_id_type=MESH,
        )

    def backward(k):
        return pltpu.make_async_remote_copy(
            src_ref=results.at[k],
            dst_ref=returns.at[k],
            send_sem=back_send.at[k],
            recv_sem=back_recv.at[k],
            device_id={"ctx": from_peer(k)},
            device_id_type=MESH,
        )

    for chunk in range(NX):
        first = chunk * NY
        packed = jnp.dot(
            held[first * SLOTS : (first + NY) * SLOTS], normed, preferred_element_type=jnp.float32
        )
        packed = packed.astype(jnp.bfloat16).reshape(NY, SLOTS, width)
        outbox[first : first + NY] = packed
        if chunk == 0:
            inbox[0] = packed[0]

        @pl.loop(max(first, 1), first + NY)
        def _(k):
            outward(k).start()

    logits = logit_cap * jnp.tanh(contract_last(router[...], normed) / logit_cap)
    plan = jnp.exp(logits)
    plan = plan / jnp.sum(plan, 0, keepdims=True)
    plans[0] = plan.astype(jnp.bfloat16)

    def plan_column(dy):
        return pltpu.make_async_remote_copy(
            src_ref=plans.at[0],
            dst_ref=plans.at[dy],
            send_sem=plan_send.at[dy],
            recv_sem=plan_recv.at[dy],
            device_id={"ctx": shifted(me, 0, dy)},
            device_id_type=MESH,
        )

    def plan_row(dx):
        return pltpu.make_async_remote_copy(
            src_ref=plans.at[pl.ds(0, NY)],
            dst_ref=plans.at[pl.ds(dx * NY, NY)],
            send_sem=plan_send.at[NY + dx],
            recv_sem=plan_recv.at[NY + dx],
            device_id={"ctx": shifted(me, dx, 0)},
            device_id_type=MESH,
        )

    for dy in range(1, NY):
        plan_column(dy).start()

    for load in loads:
        load.wait()

    @pl.loop(0, NX)
    def _(chunk):
        first = chunk * NY

        @pl.loop(jnp.maximum(first, 1), first + NY)
        def _(k):
            outward(k).wait_recv()

        block = inbox[pl.ds(first, NY)].reshape(NY * SLOTS, width)
        gate = jnp.dot(block, gate_w[...], preferred_element_type=jnp.float32)
        upward = jnp.dot(block, up_w[...], preferred_element_type=jnp.float32)
        hidden = (gate / (1.0 + jnp.exp(-gate)) * upward).astype(jnp.bfloat16)
        given = jnp.dot(hidden, down_w[...], preferred_element_type=jnp.float32)
        results[pl.ds(first, NY)] = given.astype(jnp.bfloat16).reshape(NY, SLOTS, width)

        @pl.loop(jnp.maximum(first, 1), first + NY)
        def _(k):
            backward(k).start()

        @pl.when(chunk == 1)
        def _():
            for dy in range(1, NY):
                plan_column(dy).wait_recv()
            for dx in range(1, NX):
                plan_row(dx).start()

    returns[0] = results[0]

    for dx in range(1, NX):
        plan_row(dx).wait_recv()

    target = float(rows * PEERS * 2 / experts)

    def column_sums(scale):
        def add(s, total):
            block = plans[s].astype(jnp.float32)
            if scale is None:
                return total + block
            return total + block * (2.0 / jnp.sum(block * scale, 0, keepdims=True))

        total = lax.fori_loop(0, PEERS, add, jnp.zeros((experts, rows), jnp.float32), unroll=4)
        return jnp.sum(total, 1, keepdims=True)

    scale = target / column_sums(None)
    scale = lax.fori_loop(0, ITERS - 1, lambda _, s: target / column_sums(s), scale)
    plan = plan * scale
    plan = plan * (2.0 / jnp.sum(plan, 0, keepdims=True))
    named = lax.broadcasted_iota(jnp.int32, (experts, rows), 0)
    mass = [
        jnp.sum(jnp.where(named == picked[j : j + 1], plan, 0.0), 0, keepdims=True)
        for j in range(2)
    ]
    total = mass[0] + mass[1]
    gates = jnp.where(chosen[0], mass[0] / total, 0.0) + jnp.where(chosen[1], mass[1] / total, 0.0)
    mixing = jnp.where(place[:, None, :] == slot, gates[:, None, :], 0.0)
    mixing = mixing.reshape(PEERS * SLOTS, rows).T
    high = mixing.astype(jnp.bfloat16)
    low = (mixing - high.astype(jnp.float32)).astype(jnp.bfloat16)

    @pl.loop(1, PEERS)
    def _(k):
        backward(k).wait_recv()

    step = 512
    for first in range(0, width, step):
        columns = pl.ds(first, step)
        block = returns[:, :, columns].reshape(PEERS * SLOTS, step)
        mixture = jnp.dot(high, block, preferred_element_type=jnp.float32) + jnp.dot(
            low, block, preferred_element_type=jnp.float32
        )
        layer[:, columns] = (resid[:, columns].astype(jnp.float32) + mixture).astype(jnp.bfloat16)

    for part in range(3):
        for dx in range(1, NX):
            to_head(dx, part).wait_send()

    @pl.loop(1, 4)
    def _(step):
        @pl.loop(0, NX)
        def _(i):
            ring(True, step, i).wait_send()
            ring(False, step, i).wait_send()

    @pl.loop(0, 2)
    def _(i):
        ring(True, jnp.int32(4), i).wait_send()
        ring(False, jnp.int32(4), i + 2).wait_send()

    @pl.loop(1, NX)
    def _(dx):
        give(dx).wait_send()

    @pl.loop(1, PEERS)
    def _(k):
        outward(k).wait_send()
        backward(k).wait_send()

    for dy in range(1, NY):
        plan_column(dy).wait_send()
    for dx in range(1, NX):
        plan_row(dx).wait_send()


def per_device(tokens, queries, keys, values, norm_gain, router, w_gate, w_up, w_down, picks):
    rows, width = tokens.shape
    hidden = w_gate.shape[-1]
    experts = router.shape[1]
    whole = pl.BlockSpec(memory_space=pltpu.VMEM)
    apart = pl.BlockSpec(memory_space=pl.ANY)
    box = pltpu.VMEM((PEERS, SLOTS, width), jnp.bfloat16)
    sems = pltpu.SemaphoreType.DMA
    heads_of_block = pltpu.VMEM((NX, GROUP, rows, HEAD_DIM), jnp.bfloat16)
    running = pltpu.VMEM((NX, GROUP * rows, HEAD_DIM), jnp.float32)
    return pl.pallas_call(
        layer_kernel,
        out_shape=jax.ShapeDtypeStruct((rows, width), jnp.bfloat16),
        in_specs=[whole] * 4 + [apart] * 6,
        out_specs=whole,
        scratch_shapes=[
            pltpu.VMEM((width, hidden), jnp.bfloat16),
            pltpu.VMEM((width, hidden), jnp.bfloat16),
            pltpu.VMEM((hidden, width), jnp.bfloat16),
            pltpu.VMEM((NX, rows, GROUP * HEAD_DIM), jnp.bfloat16),
            pltpu.VMEM((NX, NY, 2, rows, HEAD_DIM), jnp.bfloat16),
            running,
            running,
            heads_of_block,
            heads_of_block,
            pltpu.VMEM((rows, width), jnp.bfloat16),
            pltpu.VMEM((PEERS * SLOTS, rows), jnp.bfloat16),
            box,
            box,
            box,
            box,
            pltpu.VMEM((PEERS, experts, rows), jnp.bfloat16),
            sems((3,)),
            sems((3,)),
            sems((NX, 3)),
            sems((NX, 3)),
            sems((2, 5, NX)),
            sems((2, 5, NX)),
            sems((NX,)),
            sems((NX,)),
            sems((NY + NX,)),
            sems((NY + NX,)),
            sems((PEERS,)),
            sems((PEERS,)),
            sems((PEERS,)),
            sems((PEERS,)),
        ],
        compiler_params=pltpu.CompilerParams(
            collective_id=1, has_side_effects=True, vmem_limit_bytes=VMEM_LIMIT
        ),
        name="layer",
    )(
        tokens,
        norm_gain.reshape(1, width),
        router.T,
        picks.T,
        queries,
        keys,
        values,
        w_gate[0],
        w_up[0],
        w_down[0],
    )


def solution(mesh):
    placed = (
        P(("seq", "ctx"), None),
        P(("seq", "ctx"), None),
        P(("seq", "ctx"), None),
        P(("seq", "ctx"), None),
        P(),
        P(),
        P("ctx", None, None),
        P("ctx", None, None),
        P("ctx", None, None),
        P(("seq", "ctx"), None),
    )
    return jax.shard_map(
        per_device, mesh=mesh, in_specs=placed, out_specs=P(("seq", "ctx"), None), check_vma=False
    )
```

time: 326 us -> 113 us (0.35)
  the two profiles are of different devices: /device:TPU:6 before, /device:TPU:384 now
where the time goes in v2:
time: 113 us; the launch traced here: 112 us
  Pallas kernels  102 us (90%)
  local copies, waits for them, and re-layouts  10.1 us (9%)
    pallas_call x1, Pallas kernels, per_device(): pl.pallas_call(layer_kernel, out_shape=jax.ShapeDtypeStruct((rows, width)...  102 us
    unnamed x17, local copies, waits for them, and re-layouts  9.45 us

profile of v2, /device:TPU:384, one launch (start us, length us, event | category | flops | bytes accessed | tf_op | source)
XLA Modules:
  0.0 112.2 jit_solution(4498695279647118357)
XLA Ops:
  0.0 0.7 reshape.3.gain
  0.7 0.0 copy-start
  0.7 1.6 %copy-done = bf16[1,2048,512]{2,1,0:T(8,128)(2,1)S(1)} copy-done((bf16[1,2048,512]{2,1,0:T(8,128)(2,1)S(1)}, bf16[1,2048,512]{2,1,0:T(8,128)(2,1)}, u32[]{:S(2)}) %copy-start) | copy-done | bytes 2097176
  2.3 0.0 copy-start.1
  2.3 1.6 %copy-done.1 = bf16[1,2048,512]{2,1,0:T(8,128)(2,1)S(1)} copy-done((bf16[1,2048,512]{2,1,0:T(8,128)(2,1)S(1)}, bf16[1,2048,512]{2,1,0:T(8,128)(2,1)}, u32[]{:S(2)}) %copy-start.1) | copy-done | bytes 2097176
  3.9 0.0 copy-start.2
  3.9 1.0 copy-done.2
  4.9 0.0 copy-start.3
  4.9 1.0 copy-done.3
  6.0 0.0 copy-start.4
  6.0 0.9 copy-done.4
  6.9 0.0 copy-start.5
  6.9 0.9 copy-done.5
  7.8 0.0 copy-start.6
  7.8 0.9 copy-done.6
  8.7 0.0 copy-start.7
  8.7 0.7 copy-done.7
  9.4 102.0 %layer.1 = bf16[128,2048]{1,0:T(8,128)(2,1)S(1)} custom-call(bf16[128,2048]{1,0:T(8,128)(2,1)S(1)} %copy-done.2, bf16[1,2048]{1,0:T(2,128)(2,1)S(1)} %reshape.3.gain, bf16[32,2048]{1,0:T(8,128)(2,1)S(1)} %bitcast.7, s32[2,128]{1,0:T(2,128)S(1)} %bitcast.8, bf16[128,2048]{1,0:T(8,128)(2,1)S(1)} %copy-done.3, bf16[128,512]{1,0:T(8,128)(2,1)S(1)} %copy-done.5, ...), custom_call_target="tpu_custom_call" | custom-call | tf_op jit(solution)/shard_map/layer/pallas_call | solution.py:547
  111.4 0.8 copy.12
Async XLA Ops:
  0.7 1.6 %copy-start = (bf16[1,2048,512]{2,1,0:T(8,128)(2,1)S(1)}, bf16[1,2048,512]{2,1,0:T(8,128)(2,1)}, u32[]{:S(2)}) copy-start(bf16[1,2048,512]{2,1,0:T(8,128)(2,1)} %param.16) | copy-start | bytes 6291460
  2.3 1.6 %copy-start.1 = (bf16[1,2048,512]{2,1,0:T(8,128)(2,1)S(1)}, bf16[1,2048,512]{2,1,0:T(8,128)(2,1)}, u32[]{:S(2)}) copy-start(bf16[1,2048,512]{2,1,0:T(8,128)(2,1)} %param.17) | copy-start | bytes 6291460
  3.9 1.0 copy-start.2
  4.9 1.0 copy-start.3
  6.0 0.9 copy-start.4
  6.9 0.9 copy-start.5
  7.8 0.9 copy-start.6
  8.7 0.7 copy-start.7

commit v3 on v2

--- a/solution.py
+++ b/solution.py
@@ -17,7 +17,8 @@
 NY = 8
 PEERS = NX * NY
 SLOTS = 8
-VMEM_LIMIT = 48 * 1024 * 1024
+HEADS_AT_ONCE = 4
+VMEM_LIMIT = 60 * 1024 * 1024
 
 
 score_cap = 50.0
@@ -36,10 +37,10 @@
 
 
 def layer_kernel(
-    tokens,
-    gain,
-    router,
-    picks,
+    tokens_in,
+    gain_in,
+    router_in,
+    picks_in,
     queries,
     keys,
     values,
@@ -47,6 +48,10 @@
     w_up,
     w_down,
     layer,
+    tokens,
+    gain,
+    router,
+    picks,
     gate_w,
     up_w,
     down_w,
@@ -63,6 +68,7 @@
     results,
     returns,
     plans,
+    small_sem,
     weight_sem,
     own_sem,
     head_send,
@@ -97,6 +103,15 @@
     def _(k):
         pl.semaphore_signal(barrier, inc=1, device_id={"ctx": to_peer(k)}, device_id_type=MESH)
 
+    smalls = [
+        pltpu.make_async_copy(src, dst, small_sem.at[i])
+        for i, (src, dst) in enumerate(
+            ((picks_in, picks), (tokens_in, tokens), (gain_in, gain), (router_in, router))
+        )
+    ]
+    for small in smalls:
+        small.start()
+
     def head_columns(head):
         return pl.ds(pl.multiple_of(head * HEAD_DIM, HEAD_DIM), HEAD_DIM)
 
@@ -104,8 +119,8 @@
         return pl.ds(pl.multiple_of(head * group_width, group_width), group_width)
 
     own = [
-        (keys.at[:, head_columns(my_x)], pairs.at[my_x, 0, 0]),
-        (values.at[:, head_columns(my_x)], pairs.at[my_x, 0, 1]),
+        (keys.at[:, head_columns(my_x)], pairs.at[0, my_x, 0]),
+        (values.at[:, head_columns(my_x)], pairs.at[0, my_x, 1]),
         (queries.at[:, group_columns(my_x)], query_rows.at[my_x]),
     ]
     own = [pltpu.make_async_copy(src, dst, own_sem.at[i]) for i, (src, dst) in enumerate(own)]
@@ -124,7 +139,7 @@
             src, dst = queries.at[:, group_columns(head)], query_rows.at[my_x]
         else:
             src = (keys, values)[part].at[:, head_columns(head)]
-            dst = pairs.at[my_x, 0, part]
+            dst = pairs.at[0, my_x, part]
         return pltpu.make_async_remote_copy(
             src_ref=src,
             dst_ref=dst,
@@ -136,7 +151,7 @@
 
     def from_head(dx, part):
         source = lax.rem(my_x - dx + NX, NX)
-        dst = query_rows.at[source] if part == 2 else pairs.at[source, 0, part]
+        dst = query_rows.at[source] if part == 2 else pairs.at[0, source, part]
         return pltpu.make_async_remote_copy(
             src_ref=dst,
             dst_ref=dst,
@@ -151,6 +166,7 @@
         for dx in range(1, NX):
             to_head(dx, part).start()
 
+    smalls[0].wait()
     picked = picks[...]
     offset = lax.rem(picked // NY - my_x + NX, NX) * NY + lax.rem(
         lax.rem(picked, NY) - my_y + NY, NY
@@ -170,9 +186,6 @@
     rows_held = jnp.where(place[:, None, :] == slot, 1.0, 0.0).reshape(PEERS * SLOTS, rows)
     held[...] = rows_held.astype(jnp.bfloat16)
 
-    summed[...] = jnp.zeros_like(summed)
-    denoms[...] = jnp.zeros_like(denoms)
-
     def behind(step):
         return lax.select(step == 0, 0, 2 * step - 1)
 
@@ -184,8 +197,8 @@
         place_of = behind if up else ahead
         way = 0 if up else 1
         return pltpu.make_async_remote_copy(
-            src_ref=pairs.at[block, place_of(step - 1)],
-            dst_ref=pairs.at[block, place_of(step)],
+            src_ref=pairs.at[place_of(step - 1), block],
+            dst_ref=pairs.at[place_of(step), block],
             send_sem=ring_send.at[way, step, i],
             recv_sem=ring_recv.at[way, step, i],
             device_id={"ctx": shifted(me, 0, 1 if up else -1)},
@@ -203,71 +216,45 @@
         def _():
             ring(False, step + 1, i).start()
 
-    def attend(q_block, key_block, value_block, diagonal=False):
-        block = query_rows[q_block]
-        query = jnp.concatenate(
-            [block[:, h * HEAD_DIM : (h + 1) * HEAD_DIM] for h in range(GROUP)], 0
-        )
-        scores = contract_last(query, key_block)
-        weights = jnp.exp2(
-            jnp.tanh(scores * (1.0 / (score_cap * math.sqrt(HEAD_DIM))))
-            * (score_cap * math.log2(math.e))
-        )
-        if diagonal:
-            row = lax.broadcasted_iota(jnp.int32, (GROUP, rows, rows), 1)
-            column = lax.broadcasted_iota(jnp.int32, (GROUP, rows, rows), 2)
-            visible = (column <= row).reshape(GROUP * rows, rows)
-            weights = jnp.where(visible, weights, 0.0)
-        part = weights[:, :rows]
-        for first in range(rows, weights.shape[1], rows):
-            part = part + weights[:, first : first + rows]
-        denoms[q_block] += part
-        summed[q_block] += jnp.dot(
-            weights.astype(jnp.bfloat16), value_block, preferred_element_type=jnp.float32
-        )
-
-    def unit(block, where):
-        return pairs[block, where, 0], pairs[block, where, 1]
-
-    def attend_own(i):
-        block = lax.rem(my_x - i + NX, NX)
-        own_keys, own_values = unit(block, 0)
-        attend(block, own_keys, own_values, diagonal=True)
-
-        @pl.loop(block + 1, NX)
-        def _(q_block):
-            attend(q_block, own_keys, own_values)
-
-    def attend_two(step, i):
-        block = lax.rem(my_x - i + NX, NX)
-
-        @pl.when(my_y >= step)
-        def _():
-            attend(block, *unit(block, 2 * step - 1))
-
-        @pl.when(my_y >= NY - step)
-        def _():
-            attend(block, *unit(block, 2 * step))
-
-        @pl.loop(block + 1, NX)
-        def _(q_block):
-            first, second = unit(block, 2 * step - 1), unit(block, 2 * step)
-            attend(
-                q_block,
-                jnp.concatenate([first[0], second[0]], 0),
-                jnp.concatenate([first[1], second[1]], 0),
+    def attend(q_block, first, count, step):
+        blocks = q_block + 1
+        units = pairs[pl.ds(first, count), :blocks]
+        key_block = units[:, :, 0].reshape(count * blocks * rows, HEAD_DIM)
+        value_block = units[:, :, 1].reshape(count * blocks * rows, HEAD_DIM)
+        for first_head in range(0, GROUP, HEADS_AT_ONCE):
+            heads = range(first_head, first_head + HEADS_AT_ONCE)
+            query = [query_rows[q_block, :, h * HEAD_DIM : (h + 1) * HEAD_DIM] for h in heads]
+            query = jnp.concatenate(query, 0)
+            scores = contract_last(query, key_block)
+            weights = jnp.exp2(
+                jnp.tanh(scores * (1.0 / (score_cap * math.sqrt(HEAD_DIM))))
+                * (score_cap * math.log2(math.e))
             )
-
-    def attend_opposite(i):
-        block = lax.rem(my_x - i + NX, NX)
-
-        @pl.when(my_y >= NY // 2)
-        def _():
-            attend(block, *unit(block, 7))
-
-        @pl.loop(block + 1, NX)
-        def _(q_block):
-            attend(q_block, *unit(block, 7))
+            parts = [weights[:, c : c + rows] for c in range(0, weights.shape[1], rows)]
+            if step is None:
+                shape = (HEADS_AT_ONCE, rows, rows)
+                row = lax.broadcasted_iota(jnp.int32, shape, 1)
+                column = lax.broadcasted_iota(jnp.int32, shape, 2)
+                visible = [(column <= row).reshape(HEADS_AT_ONCE * rows, rows)]
+            elif count == 2:
+                visible = [my_y >= step, my_y >= NY - step]
+            else:
+                visible = [my_y >= step]
+            for c, seen in enumerate(visible):
+                c = c * blocks + q_block
+                parts[c] = jnp.where(seen, parts[c], 0.0)
+            here = pl.ds(first_head * rows, HEADS_AT_ONCE * rows)
+            total = parts[0]
+            for part in parts[1:]:
+                total = total + part
+            rounded = jnp.concatenate([part.astype(jnp.bfloat16) for part in parts], 1)
+            given = jnp.dot(rounded, value_block, preferred_element_type=jnp.float32)
+            if step is None:
+                denoms[q_block, here] = total
+                summed[q_block, here] = given
+            else:
+                denoms[q_block, here] += total
+                summed[q_block, here] += given
 
     for copy in own[:2]:
         copy.wait()
@@ -285,34 +272,22 @@
         ring(False, step, i).wait_recv()
         forward(step, i)
 
-    @pl.loop(0, NX)
-    def _(i):
+    for i in range(NX):
         arrive(jnp.int32(1), i)
-        attend_own(i)
+        attend(i, 0, 1, None)
 
     @pl.loop(2, 4)
     def _(step):
-        @pl.loop(0, NX)
-        def _(i):
+        for i in range(NX):
             arrive(step, i)
-            attend_two(step - 1, i)
-
-    @pl.loop(0, NX)
-    def _(i):
-        attend_two(3, i)
-
-        @pl.when(i < 2)
-        def _():
-            ring(True, jnp.int32(4), i).wait_recv()
-
-        @pl.when(i >= 2)
-        def _():
-            ring(False, jnp.int32(4), i).wait_recv()
-
-        attend_opposite(i)
-
-    def give(dx):
-        block = lax.rem(my_x + dx, NX)
+            attend(i, 2 * step - 3, 2, step - 1)
+
+    for i in range(NX):
+        attend(i, 5, 2, 3)
+        ring(i < 2, jnp.int32(4), i).wait_recv()
+
+    def give(block):
+        dx = lax.rem(block - my_x + NX, NX)
         return pltpu.make_async_remote_copy(
             src_ref=finished.at[block],
             dst_ref=attended.at[my_x],
@@ -333,22 +308,25 @@
             device_id_type=MESH,
         )
 
-    def normal(block):
+    for block in range(NX):
+        attend(block, 7, 1, 4)
         denom = jnp.sum(denoms[block], -1, keepdims=True)
-        return (summed[block] / denom).astype(jnp.bfloat16).reshape(GROUP, rows, HEAD_DIM)
-
-    @pl.loop(1, NX)
-    def _(dx):
-        block = lax.rem(my_x + dx, NX)
-        finished[block] = normal(block)
-        give(dx).start()
-
-    attended[my_x] = normal(my_x)
+        finished[block] = (
+            (summed[block] / denom).astype(jnp.bfloat16).reshape(GROUP, rows, HEAD_DIM)
+        )
+
+        @pl.when(my_x != block)
+        def _():
+            give(block).start()
+
+    attended[my_x] = finished[my_x]
 
     @pl.loop(1, NX)
     def _(dx):
         take(dx).wait_recv()
 
+    for small in smalls[1:]:
+        small.wait()
     square = jnp.zeros((rows, HEAD_DIM), jnp.float32)
     for h in range(HEADS):
         columns = slice(h * HEAD_DIM, (h + 1) * HEAD_DIM)
@@ -363,7 +341,7 @@
     normed = (
         resid[...].astype(jnp.float32)
         * lax.rsqrt(mean_square + epsilon)
-        * gain[...].astype(jnp.float32)
+        * gain[...].astype(jnp.float32).reshape(1, width)
     ).astype(jnp.bfloat16)
 
     def outward(k):
@@ -521,7 +499,7 @@
 
     @pl.loop(1, NX)
     def _(dx):
-        give(dx).wait_send()
+        give(lax.rem(my_x + dx, NX)).wait_send()
 
     @pl.loop(1, PEERS)
     def _(k):
@@ -539,7 +517,7 @@
     hidden = w_gate.shape[-1]
     experts = router.shape[1]
     whole = pl.BlockSpec(memory_space=pltpu.VMEM)
-    apart = pl.BlockSpec(memory_space=pl.ANY)
+    apart = pl.BlockSpec(memory_space=pltpu.HBM)
     box = pltpu.VMEM((PEERS, SLOTS, width), jnp.bfloat16)
     sems = pltpu.SemaphoreType.DMA
     heads_of_block = pltpu.VMEM((NX, GROUP, rows, HEAD_DIM), jnp.bfloat16)
@@ -547,14 +525,18 @@
     return pl.pallas_call(
         layer_kernel,
         out_shape=jax.ShapeDtypeStruct((rows, width), jnp.bfloat16),
-        in_specs=[whole] * 4 + [apart] * 6,
+        in_specs=[apart] * 10,
         out_specs=whole,
         scratch_shapes=[
+            pltpu.VMEM((rows, width), jnp.bfloat16),
+            pltpu.VMEM((width,), jnp.bfloat16),
+            pltpu.VMEM((experts, width), jnp.bfloat16),
+            pltpu.VMEM((2, rows), jnp.int32),
             pltpu.VMEM((width, hidden), jnp.bfloat16),
             pltpu.VMEM((width, hidden), jnp.bfloat16),
             pltpu.VMEM((hidden, width), jnp.bfloat16),
             pltpu.VMEM((NX, rows, GROUP * HEAD_DIM), jnp.bfloat16),
-            pltpu.VMEM((NX, NY, 2, rows, HEAD_DIM), jnp.bfloat16),
+            pltpu.VMEM((NY, NX, 2, rows, HEAD_DIM), jnp.bfloat16),
             running,
             running,
             heads_of_block,
@@ -566,6 +548,7 @@
             box,
             box,
             pltpu.VMEM((PEERS, experts, rows), jnp.bfloat16),
+            sems((4,)),
             sems((3,)),
             sems((3,)),
             sems((NX, 3)),
@@ -587,7 +570,7 @@
         name="layer",
     )(
         tokens,
-        norm_gain.reshape(1, width),
+        norm_gain,
         router.T,
         picks.T,
         queries,

time: 113 us -> 98.3 us (0.87)
  the two profiles are of different devices: /device:TPU:384 before, /device:TPU:512 now
where the time goes in v3:
time: 98.3 us; the launch traced here: 98.1 us
  Pallas kernels  96.2 us (98%)
  local copies, waits for them, and re-layouts  1.88 us (2%)
    pallas_call x1, Pallas kernels, per_device(): pl.pallas_call(layer_kernel, out_shape=jax.ShapeDtypeStruct((rows, width)...  96.2 us

profile of v3, /device:TPU:512, one launch (start us, length us, event | category | flops | bytes accessed | tf_op | source)
XLA Modules:
  0.0 98.1 jit_solution(17287046284186350708)
XLA Ops:
  0.0 96.2 %layer.1 = bf16[128,2048]{1,0:T(8,128)(2,1)} custom-call(bf16[128,2048]{1,0:T(8,128)(2,1)} %tokens_in.1, bf16[2048]{0:T(1024)(128)(2,1)} %gain_in.1, bf16[32,2048]{1,0:T(8,128)(2,1)} %bitcast.8, s32[2,128]{1,0:T(2,128)} %bitcast.9, bf16[128,2048]{1,0:T(8,128)(2,1)} %queries.1, bf16[128,512]{1,0:T(8,128)(2,1)} %keys.1, bf16[128,512]{1,0:T(8,128)(2,1)} %values.1, ...), custom_call_target="tpu_custom_call" | custom-call | tf_op jit(solution)/shard_map/layer/pallas_call | solution.py:525
  96.3 1.9 %copy.12 = bf16[128,2048]{1,0:T(8,128)(2,1)} copy(bf16[128,2048]{1,0:T(8,128)(2,1)} %layer.1) | data formatting | bytes 1048576

commit v4 on v3

--- a/solution.py
+++ b/solution.py
@@ -17,6 +17,7 @@
 NY = 8
 PEERS = NX * NY
 SLOTS = 8
+MIX_WIDTH = 512
 HEADS_AT_ONCE = 4
 VMEM_LIMIT = 60 * 1024 * 1024
 
@@ -63,6 +64,7 @@
     attended,
     resid,
     held,
+    mixed,
     outbox,
     inbox,
     results,
@@ -99,9 +101,9 @@
 
     barrier = pltpu.get_barrier_semaphore()
 
-    @pl.loop(1, PEERS)
-    def _(k):
-        pl.semaphore_signal(barrier, inc=1, device_id={"ctx": to_peer(k)}, device_id_type=MESH)
+    near = [shifted(me, dx, 0) for dx in range(1, NX)] + [shifted(me, 0, dy) for dy in (1, -1)]
+    for peer in near:
+        pl.semaphore_signal(barrier, inc=1, device_id={"ctx": peer}, device_id_type=MESH)
 
     smalls = [
         pltpu.make_async_copy(src, dst, small_sem.at[i])
@@ -161,9 +163,9 @@
             device_id_type=MESH,
         )
 
-    pl.semaphore_wait(barrier, PEERS - 1)
-    for part in range(3):
-        for dx in range(1, NX):
+    pl.semaphore_wait(barrier, len(near))
+    for dx in range(1, NX):
+        for part in range(2):
             to_head(dx, part).start()
 
     smalls[0].wait()
@@ -263,6 +265,8 @@
         from_head(dx, 0).wait_recv()
         from_head(dx, 1).wait_recv()
         forward(0, dx)
+    for dx in range(1, NX):
+        to_head(dx, 2).start()
     own[2].wait()
     for dx in range(1, NX):
         from_head(dx, 2).wait_recv()
@@ -468,19 +472,6 @@
     high = mixing.astype(jnp.bfloat16)
     low = (mixing - high.astype(jnp.float32)).astype(jnp.bfloat16)
 
-    @pl.loop(1, PEERS)
-    def _(k):
-        backward(k).wait_recv()
-
-    step = 512
-    for first in range(0, width, step):
-        columns = pl.ds(first, step)
-        block = returns[:, :, columns].reshape(PEERS * SLOTS, step)
-        mixture = jnp.dot(high, block, preferred_element_type=jnp.float32) + jnp.dot(
-            low, block, preferred_element_type=jnp.float32
-        )
-        layer[:, columns] = (resid[:, columns].astype(jnp.float32) + mixture).astype(jnp.bfloat16)
-
     for part in range(3):
         for dx in range(1, NX):
             to_head(dx, part).wait_send()
@@ -504,12 +495,41 @@
     @pl.loop(1, PEERS)
     def _(k):
         outward(k).wait_send()
-        backward(k).wait_send()
 
     for dy in range(1, NY):
         plan_column(dy).wait_send()
     for dx in range(1, NX):
         plan_row(dx).wait_send()
+
+    def mix(k, first, last):
+        columns = pl.ds(first, MIX_WIDTH)
+        block = returns[k:last, :, columns].reshape((last - k) * SLOTS, MIX_WIDTH)
+        here = slice(k * SLOTS, last * SLOTS)
+        return jnp.dot(high[:, here], block, preferred_element_type=jnp.float32) + jnp.dot(
+            low[:, here], block, preferred_element_type=jnp.float32
+        )
+
+    most = PEERS // 2
+
+    @pl.loop(1, most)
+    def _(k):
+        backward(k).wait_recv()
+
+    for first in range(0, width, MIX_WIDTH):
+        columns = pl.ds(first, MIX_WIDTH)
+        mixed[:, columns] = resid[:, columns].astype(jnp.float32) + mix(0, first, most)
+
+    @pl.loop(most, PEERS)
+    def _(k):
+        backward(k).wait_recv()
+
+    for first in range(0, width, MIX_WIDTH):
+        columns = pl.ds(first, MIX_WIDTH)
+        layer[:, columns] = (mixed[:, columns] + mix(most, first, PEERS)).astype(jnp.bfloat16)
+
+    @pl.loop(1, PEERS)
+    def _(k):
+        backward(k).wait_send()
 
 
 def per_device(tokens, queries, keys, values, norm_gain, router, w_gate, w_up, w_down, picks):
@@ -543,6 +563,7 @@
             heads_of_block,
             pltpu.VMEM((rows, width), jnp.bfloat16),
             pltpu.VMEM((PEERS * SLOTS, rows), jnp.bfloat16),
+            pltpu.VMEM((rows, width), jnp.float32),
             box,
             box,
             box,

time: 98.3 us -> 96.8 us (0.985)
  the two profiles are of different devices: /device:TPU:512 before, /device:TPU:328 now
where the time goes in v4:
time: 96.8 us; the launch traced here: 96.6 us
  Pallas kernels  94.7 us (98%)
  local copies, waits for them, and re-layouts  1.88 us (2%)
    pallas_call x1, Pallas kernels, per_device(): pl.pallas_call(layer_kernel, out_shape=jax.ShapeDtypeStruct((rows, width)...  94.7 us

profile of v4, /device:TPU:328, one launch (start us, length us, event | category | flops | bytes accessed | tf_op | source)
XLA Modules:
  0.0 96.6 jit_solution(7866339434413464885)
XLA Ops:
  0.0 94.7 %layer.1 = bf16[128,2048]{1,0:T(8,128)(2,1)} custom-call(bf16[128,2048]{1,0:T(8,128)(2,1)} %tokens_in.1, bf16[2048]{0:T(1024)(128)(2,1)} %gain_in.1, bf16[32,2048]{1,0:T(8,128)(2,1)} %bitcast.8, s32[2,128]{1,0:T(2,128)} %bitcast.9, bf16[128,2048]{1,0:T(8,128)(2,1)} %queries.1, bf16[128,512]{1,0:T(8,128)(2,1)} %keys.1, bf16[128,512]{1,0:T(8,128)(2,1)} %values.1, ...), custom_call_target="tpu_custom_call" | custom-call | tf_op jit(solution)/shard_map/layer/pallas_call | solution.py:545
  94.7 1.9 %copy.12 = bf16[128,2048]{1,0:T(8,128)(2,1)} copy(bf16[128,2048]{1,0:T(8,128)(2,1)} %layer.1) | data formatting | bytes 1048576

commit v5 on v4

--- a/solution.py
+++ b/solution.py
@@ -65,8 +65,11 @@
     resid,
     held,
     mixed,
-    outbox,
-    inbox,
+    first_out,
+    rest_out,
+    first_in,
+    rest_in,
+    landed,
     results,
     returns,
     plans,
@@ -323,40 +326,55 @@
         def _():
             give(block).start()
 
-    attended[my_x] = finished[my_x]
-
-    @pl.loop(1, NX)
-    def _(dx):
-        take(dx).wait_recv()
-
     for small in smalls[1:]:
         small.wait()
-    square = jnp.zeros((rows, HEAD_DIM), jnp.float32)
-    for h in range(HEADS):
-        columns = slice(h * HEAD_DIM, (h + 1) * HEAD_DIM)
+
+    def stream_of(group, heads):
+        columns = group_columns(group)
+        attended_columns = jnp.concatenate([heads[h] for h in range(GROUP)], 1)
         stream = (
-            tokens[:, columns].astype(jnp.float32)
-            + attended[h // GROUP, h % GROUP].astype(jnp.float32)
+            tokens[:, columns].astype(jnp.float32) + attended_columns.astype(jnp.float32)
         ).astype(jnp.bfloat16)
         resid[:, columns] = stream
-        stream = stream.astype(jnp.float32)
-        square = square + stream * stream
-    mean_square = jnp.sum(square, -1, keepdims=True) / width
-    normed = (
-        resid[...].astype(jnp.float32)
-        * lax.rsqrt(mean_square + epsilon)
-        * gain[...].astype(jnp.float32).reshape(1, width)
-    ).astype(jnp.bfloat16)
-
-    def outward(k):
-        return pltpu.make_async_remote_copy(
-            src_ref=outbox.at[k],
-            dst_ref=inbox.at[k],
-            send_sem=out_send.at[k],
-            recv_sem=out_recv.at[k],
+        packed = jnp.dot(held[...], stream, preferred_element_type=jnp.float32)
+        return packed.astype(jnp.bfloat16).reshape(PEERS, SLOTS, group_width)
+
+    def outward(k, part):
+        return pltpu.make_async_remote_copy(
+            src_ref=(first_out, rest_out)[part].at[k],
+            dst_ref=(first_in, rest_in)[part].at[k],
+            send_sem=out_send.at[part, k],
+            recv_sem=out_recv.at[part, k],
             device_id={"ctx": to_peer(k)},
             device_id_type=MESH,
         )
+
+    first_out[...] = stream_of(my_x, finished[my_x])
+
+    @pl.loop(1, PEERS)
+    def _(k):
+        outward(k, 0).start()
+
+    first_in[0] = first_out[0]
+
+    for dx in range(1, NX):
+        take(dx).wait_recv()
+        source = lax.rem(my_x - dx + NX, NX)
+        rest_out[:, dx - 1] = stream_of(source, attended[source])
+
+    @pl.loop(1, PEERS)
+    def _(k):
+        outward(k, 1).start()
+
+    rest_in[0] = rest_out[0]
+
+    def norm(rows_in):
+        wide = rows_in.astype(jnp.float32)
+        mean_square = jnp.mean(wide * wide, -1, keepdims=True)
+        wide_gain = gain[...].astype(jnp.float32).reshape(1, width)
+        return (wide * lax.rsqrt(mean_square + epsilon) * wide_gain).astype(jnp.bfloat16)
+
+    normed = norm(resid[...])
 
     def backward(k):
         return pltpu.make_async_remote_copy(
@@ -368,20 +386,6 @@
             device_id_type=MESH,
         )
 
-    for chunk in range(NX):
-        first = chunk * NY
-        packed = jnp.dot(
-            held[first * SLOTS : (first + NY) * SLOTS], normed, preferred_element_type=jnp.float32
-        )
-        packed = packed.astype(jnp.bfloat16).reshape(NY, SLOTS, width)
-        outbox[first : first + NY] = packed
-        if chunk == 0:
-            inbox[0] = packed[0]
-
-        @pl.loop(max(first, 1), first + NY)
-        def _(k):
-            outward(k).start()
-
     logits = logit_cap * jnp.tanh(contract_last(router[...], normed) / logit_cap)
     plan = jnp.exp(logits)
     plan = plan / jnp.sum(plan, 0, keepdims=True)
@@ -419,9 +423,17 @@
 
         @pl.loop(jnp.maximum(first, 1), first + NY)
         def _(k):
-            outward(k).wait_recv()
-
-        block = inbox[pl.ds(first, NY)].reshape(NY * SLOTS, width)
+            outward(k, 0).wait_recv()
+            outward(k, 1).wait_recv()
+
+        source = lax.rem(my_x - chunk + NX, NX)
+        here = pl.ds(first, NY)
+        landed[:, group_columns(source)] = first_in[here].reshape(NY * SLOTS, group_width)
+        for dx in range(1, NX):
+            landed[:, group_columns(lax.rem(source - dx + NX, NX))] = rest_in[
+                here, dx - 1
+            ].reshape(NY * SLOTS, group_width)
+        block = norm(landed[...])
         gate = jnp.dot(block, gate_w[...], preferred_element_type=jnp.float32)
         upward = jnp.dot(block, up_w[...], preferred_element_type=jnp.float32)
         hidden = (gate / (1.0 + jnp.exp(-gate)) * upward).astype(jnp.bfloat16)
@@ -494,7 +506,8 @@
 
     @pl.loop(1, PEERS)
     def _(k):
-        outward(k).wait_send()
+        outward(k, 0).wait_send()
+        outward(k, 1).wait_send()
 
     for dy in range(1, NY):
         plan_column(dy).wait_send()
@@ -564,8 +577,11 @@
             pltpu.VMEM((rows, width), jnp.bfloat16),
             pltpu.VMEM((PEERS * SLOTS, rows), jnp.bfloat16),
             pltpu.VMEM((rows, width), jnp.float32),
-            box,
-            box,
+            pltpu.VMEM((PEERS, SLOTS, GROUP * HEAD_DIM), jnp.bfloat16),
+            pltpu.VMEM((PEERS, NX - 1, SLOTS, GROUP * HEAD_DIM), jnp.bfloat16),
+            pltpu.VMEM((PEERS, SLOTS, GROUP * HEAD_DIM), jnp.bfloat16),
+            pltpu.VMEM((PEERS, NX - 1, SLOTS, GROUP * HEAD_DIM), jnp.bfloat16),
+            pltpu.VMEM((NY * SLOTS, width), jnp.bfloat16),
             box,
             box,
             pltpu.VMEM((PEERS, experts, rows), jnp.bfloat16),
@@ -580,8 +596,8 @@
             sems((NX,)),
             sems((NY + NX,)),
             sems((NY + NX,)),
-            sems((PEERS,)),
-            sems((PEERS,)),
+            sems((2, PEERS)),
+            sems((2, PEERS)),
             sems((PEERS,)),
             sems((PEERS,)),
         ],

time: 96.8 us -> 93.4 us (0.965)
  the two profiles are of different devices: /device:TPU:328 before, /device:TPU:6 now
where the time goes in v5:
time: 93.4 us; the launch traced here: 93.3 us
  Pallas kernels  91.4 us (98%)
  local copies, waits for them, and re-layouts  1.88 us (2%)
    pallas_call x1, Pallas kernels, per_device(): pl.pallas_call(layer_kernel, out_shape=jax.ShapeDtypeStruct((rows, width)...  91.4 us
    unnamed x1, local copies, waits for them, and re-layouts  1.88 us

profile of v5, /device:TPU:6, one launch (start us, length us, event | category | flops | bytes accessed | tf_op | source)
XLA Modules:
  0.0 93.3 jit_solution(14965808979349128099)
XLA Ops:
  0.0 91.4 %layer.1 = bf16[128,2048]{1,0:T(8,128)(2,1)} custom-call(bf16[128,2048]{1,0:T(8,128)(2,1)} %tokens_in.1, bf16[2048]{0:T(1024)(128)(2,1)} %gain_in.1, bf16[32,2048]{1,0:T(8,128)(2,1)} %bitcast.8, s32[2,128]{1,0:T(2,128)} %bitcast.9, bf16[128,2048]{1,0:T(8,128)(2,1)} %queries.1, bf16[128,512]{1,0:T(8,128)(2,1)} %keys.1, bf16[128,512]{1,0:T(8,128)(2,1)} %values.1, ...), custom_call_target="tpu_custom_call" | custom-call | tf_op jit(solution)/shard_map/layer/pallas_call | solution.py:558
  91.4 1.9 %copy.12 = bf16[128,2048]{1,0:T(8,128)(2,1)} copy(bf16[128,2048]{1,0:T(8,128)(2,1)} %layer.1) | data formatting | bytes 1048576

commit v6 on v5

--- a/solution.py
+++ b/solution.py
@@ -114,8 +114,7 @@
             ((picks_in, picks), (tokens_in, tokens), (gain_in, gain), (router_in, router))
         )
     ]
-    for small in smalls:
-        small.start()
+    smalls[0].start()
 
     def head_columns(head):
         return pl.ds(pl.multiple_of(head * HEAD_DIM, HEAD_DIM), HEAD_DIM)
@@ -135,8 +134,6 @@
         pltpu.make_async_copy(src, dst, weight_sem.at[i])
         for i, (src, dst) in enumerate(((w_gate, gate_w), (w_up, up_w), (w_down, down_w)))
     ]
-    for load in loads:
-        load.start()
 
     def to_head(dx, part):
         head = lax.rem(my_x + dx, NX)
@@ -270,6 +267,8 @@
         forward(0, dx)
     for dx in range(1, NX):
         to_head(dx, 2).start()
+    for load in smalls[1:] + loads:
+        load.start()
     own[2].wait()
     for dx in range(1, NX):
         from_head(dx, 2).wait_recv()

time: 93.4 us -> 93.5 us (level)
  no operation moved by 1% of the time
where the time goes in v6:
time: 93.5 us; the launch traced here: 93.3 us
  Pallas kernels  91.4 us (98%)
  local copies, waits for them, and re-layouts  1.88 us (2%)
    pallas_call x1, Pallas kernels, per_device(): pl.pallas_call(layer_kernel, out_shape=jax.ShapeDtypeStruct((rows, width)...  91.4 us
    unnamed x1, local copies, waits for them, and re-layouts  1.88 us

profile of v6, /device:TPU:6, one launch (start us, length us, event | category | flops | bytes accessed | tf_op | source)
XLA Modules:
  0.0 93.3 jit_solution(5827792946787121785)
XLA Ops:
  0.0 91.4 %layer.1 = bf16[128,2048]{1,0:T(8,128)(2,1)} custom-call(bf16[128,2048]{1,0:T(8,128)(2,1)} %tokens_in.1, bf16[2048]{0:T(1024)(128)(2,1)} %gain_in.1, bf16[32,2048]{1,0:T(8,128)(2,1)} %bitcast.8, s32[2,128]{1,0:T(2,128)} %bitcast.9, bf16[128,2048]{1,0:T(8,128)(2,1)} %queries.1, bf16[128,512]{1,0:T(8,128)(2,1)} %keys.1, bf16[128,512]{1,0:T(8,128)(2,1)} %values.1, ...), custom_call_target="tpu_custom_call" | custom-call | tf_op jit(solution)/shard_map/layer/pallas_call | solution.py:557
  91.4 1.9 %copy.12 = bf16[128,2048]{1,0:T(8,128)(2,1)} copy(bf16[128,2048]{1,0:T(8,128)(2,1)} %layer.1) | data formatting | bytes 1048576
